TPU v7x, 256 devices: a whole 4x4x8 slice. The times are simulated.
256 devices in a mesh: ctx: 32 (over y, x, core), head: 8 (over z).
Axes of the slice: x: 4, y: 4, z: 8, core: 2. Of those that a mesh axis runs over, the one named last changes fastest.
Arguments:
- queries: bfloat16 [16384, 4096], P(('ctx', 'head')), may hold values from -6 to 6
- key_states: bfloat16 [16384, 1024], P(('ctx', 'head')), may hold values from -6 to 6
- value_states: bfloat16 [16384, 1024], P(('ctx', 'head')), may hold values from -6 to 6
- out_grad: bfloat16 [16384, 4096], P(('ctx', 'head')), may hold values from -6 to 6
- doc_lengths: int32 [13], replicated, may hold values from 1 to 3073, as said below
- key_first: int32 [64], replicated, may hold values from 0 to 57, as said below
- block_order: int32 [64], replicated, may hold values from 0 to 63, as said below
Outputs:
- attended: bfloat16 [16384, 4096], P('ctx', 'head')
- query_grad: bfloat16 [16384, 4096], P('ctx', 'head')
- key_grad: bfloat16 [16384, 1024], P('ctx', 'head')
- value_grad: bfloat16 [16384, 1024], P('ctx', 'head')
Inputs may be any that keep to these rules, and one draw needn't show every extreme that they name: `doc_lengths`: they sum to 16384; the last document is the longest, of 3073 tokens. key_first[b] is the later of b - 6 and the block that holds the first token of the document holding token b * 256. `block_order`: A permutation of the 64 sequence blocks.
All inputs are finite; a program needn't handle non-finite values.
Results may differ from a plain program's by a relative error of at most 0.035.
Values may be sent and summed in bfloat16 or wider, within the bound.
A program may use at most 128 MiB of HBM per device.

v0:
```python
import jax
import jax.numpy as jnp
from jax import lax
from jax.sharding import PartitionSpec as P

HD = 128
BLOCK = 256


def tile_scores(query_tile, key_tile, score_scale):
    return (
        jnp.einsum("qhgd,khd->hgqk", query_tile, key_tile, preferred_element_type=jnp.float32)
        * score_scale
    )


def permitted(query_pos, query_docs, query_first, key_pos, key_docs):
    same_doc = query_docs[:, None] == key_docs[None, :]
    causal = key_pos[None, :] <= query_pos[:, None]
    listed = key_pos[None, :] // BLOCK >= query_first[:, None]
    return same_doc & causal & listed


def on_device(queries, key_states, value_states, out_grad, doc_lengths, key_first, block_order):
    my_queries, my_keys, my_values, my_grads = (
        lax.all_to_all(queries, "head", split_axis=1, concat_axis=0, tiled=True),
        lax.all_to_all(key_states, "head", split_axis=1, concat_axis=0, tiled=True),
        lax.all_to_all(value_states, "head", split_axis=1, concat_axis=0, tiled=True),
        lax.all_to_all(out_grad, "head", split_axis=1, concat_axis=0, tiled=True),
    )
    row_count = my_queries.shape[0]
    kv_heads = my_keys.shape[1] // HD
    group_size = my_queries.shape[1] // HD // kv_heads
    tokens = row_count * lax.axis_size("ctx")
    block_count = tokens // BLOCK
    local_blocks = row_count // BLOCK
    score_scale = HD ** (-0.5)
    row_start = lax.axis_index("ctx") * row_count
    block_start = lax.axis_index("ctx") * local_blocks
    head_width = kv_heads * HD
    offsets = jnp.arange(BLOCK, dtype=jnp.int32)
    block_ids = jnp.arange(block_count, dtype=jnp.int32)
    seq_pos = (block_order[:, None] * BLOCK + offsets[None, :]).reshape(tokens)
    doc_ends = jnp.cumsum(doc_lengths)
    documents = jnp.sum((seq_pos[:, None] >= doc_ends[None, :]).astype(jnp.int32), axis=1)
    first_block = jnp.sum(
        jnp.where(block_order[:, None] == block_ids[None, :], key_first[None, :], 0), axis=1
    )
    first_rows = (first_block[:, None] + 0 * offsets[None, :]).reshape(tokens)
    my_pos = lax.dynamic_slice_in_dim(seq_pos, row_start, row_count)
    my_docs = lax.dynamic_slice_in_dim(documents, row_start, row_count)
    my_first = lax.dynamic_slice_in_dim(first_rows, row_start, row_count)
    query_tile = my_queries.reshape(row_count, kv_heads, group_size, HD)
    grad_tile = my_grads.reshape(row_count, kv_heads, group_size, HD)
    all_keys, all_values = (
        lax.all_gather(my_keys, "ctx", axis=0, tiled=True),
        lax.all_gather(my_values, "ctx", axis=0, tiled=True),
    )
    my_blocks = lax.dynamic_slice_in_dim(block_order, block_start, local_blocks)
    my_reach = lax.dynamic_slice_in_dim(first_block, block_start, local_blocks)
    needed = jnp.any(
        (block_order[:, None] >= my_reach[None, :]) & (block_order[:, None] <= my_blocks[None, :]),
        axis=1,
    )
    listed_count = jnp.sum(needed.astype(jnp.int32))
    per_turn = max(1, min(block_count, 512 // BLOCK))
    listing = jnp.argsort(jnp.where(needed, block_ids, block_count + block_ids))
    listing = jnp.concatenate([listing, listing[:per_turn]])
    turn_count = (listed_count + per_turn - 1) // per_turn

    def key_group(turn_index):
        chosen = lax.dynamic_slice_in_dim(listing, turn_index * per_turn, per_turn)
        usable = turn_index * per_turn + jnp.arange(per_turn) < listed_count
        key_parts, value_parts, pos_parts, doc_parts, flag_parts = ([], [], [], [], [])
        for slot_index in range(per_turn):
            first_row = chosen[slot_index] * BLOCK
            key_parts.append(lax.dynamic_slice_in_dim(all_keys, first_row, BLOCK))
            value_parts.append(lax.dynamic_slice_in_dim(all_values, first_row, BLOCK))
            pos_parts.append(lax.dynamic_slice_in_dim(seq_pos, first_row, BLOCK))
            doc_parts.append(lax.dynamic_slice_in_dim(documents, first_row, BLOCK))
            flag_parts.append(jnp.broadcast_to(usable[slot_index], (BLOCK,)))
        key_tile = jnp.concatenate(key_parts).reshape(per_turn * BLOCK, kv_heads, HD)
        value_tile = jnp.concatenate(value_parts).reshape(per_turn * BLOCK, kv_heads, HD)
        allowed = permitted(
            my_pos, my_docs, my_first, jnp.concatenate(pos_parts), jnp.concatenate(doc_parts)
        )
        allowed = allowed & jnp.concatenate(flag_parts)[None, :]
        return (chosen, key_tile, value_tile, allowed)

    def forward_step(turn_index, state):
        maxima, totals, running = state
        chosen, key_tile, value_tile, allowed = key_group(turn_index)
        scores = jnp.where(allowed, tile_scores(query_tile, key_tile, score_scale), -jnp.inf)
        new_maxima = jnp.maximum(maxima, jnp.max(scores, axis=-1))
        safe_maxima = jnp.where(new_maxima == -jnp.inf, 0.0, new_maxima)
        rescale = jnp.exp(maxima - safe_maxima)
        shifted = jnp.exp(scores - safe_maxima[..., None])
        totals = totals * rescale + jnp.sum(shifted, axis=-1)
        product = jnp.einsum(
            "hgqk,khd->hgqd",
            shifted.astype(jnp.bfloat16),
            value_tile,
            preferred_element_type=jnp.float32,
        )
        running = running * rescale[..., None] + product
        return (new_maxima, totals, running)

    stat_shape = (kv_heads, group_size, row_count)
    start_state = (
        jnp.full(stat_shape, -jnp.inf, jnp.float32),
        jnp.zeros(stat_shape, jnp.float32),
        jnp.zeros(stat_shape + (HD,), jnp.float32),
    )
    maxima, totals, running = lax.fori_loop(0, turn_count, forward_step, start_state)
    log_total = maxima + jnp.log(totals)
    attended = jnp.transpose(running / totals[..., None], (2, 0, 1, 3)).astype(jnp.bfloat16)
    delta = jnp.einsum("qhgd,qhgd->hgq", grad_tile, attended, preferred_element_type=jnp.float32)

    def backward_tile(turn_index):
        chosen, key_tile, value_tile, allowed = key_group(turn_index)
        scores = jnp.where(allowed, tile_scores(query_tile, key_tile, score_scale), -jnp.inf)
        probs = jnp.exp(scores - log_total[..., None])
        prob_grad = jnp.einsum(
            "qhgd,khd->hgqk", grad_tile, value_tile, preferred_element_type=jnp.float32
        )
        score_grad = (probs * (prob_grad - delta[..., None])).astype(jnp.bfloat16)
        return (chosen, key_tile, probs, score_grad)

    tile_shape = (row_count, kv_heads, group_size, HD)

    def joint_step(turn_index, state):
        running_sum, partials = state
        chosen, key_tile, probs, score_grad = backward_tile(turn_index)
        running_sum = running_sum + jnp.einsum(
            "hgqk,khd->qhgd", score_grad, key_tile, preferred_element_type=jnp.float32
        )
        key_part = (
            jnp.einsum("hgqk,qhgd->khd", score_grad, query_tile, preferred_element_type=jnp.float32)
            * score_scale
        )
        value_part = jnp.einsum(
            "hgqk,qhgd->khd",
            probs.astype(jnp.bfloat16),
            grad_tile,
            preferred_element_type=jnp.float32,
        )
        key_count = key_part.shape[0]
        joined = jnp.concatenate(
            [key_part.reshape(key_count, head_width), value_part.reshape(key_count, head_width)],
            axis=1,
        )
        for slot_index in range(per_turn):
            first_row = chosen[slot_index] * BLOCK
            current = lax.dynamic_slice_in_dim(partials, first_row, BLOCK)
            partials = lax.dynamic_update_slice_in_dim(
                partials,
                current + joined[slot_index * BLOCK : (slot_index + 1) * BLOCK],
                first_row,
                0,
            )
        return (running_sum, partials)

    start_joint = (
        jnp.zeros(tile_shape, jnp.float32),
        jnp.zeros((tokens, 2 * head_width), jnp.float32),
    )
    query_sum, partials = lax.fori_loop(0, turn_count, joint_step, start_joint)
    summed = lax.psum_scatter(
        partials.astype(jnp.bfloat16), "ctx", scatter_dimension=0, tiled=True
    ).astype(jnp.float32)
    query_grad = (
        (query_sum * score_scale)
        .astype(jnp.bfloat16)
        .reshape(row_count, kv_heads * group_size * HD)
    )
    key_grad = summed[:, :head_width].astype(jnp.bfloat16)
    value_grad = summed[:, head_width:].astype(jnp.bfloat16)
    attended_rows = attended.reshape(row_count, kv_heads * group_size * HD)
    return (attended_rows, query_grad, key_grad, value_grad)


def solution(mesh):
    return jax.shard_map(
        on_device,
        mesh=mesh,
        in_specs=(
            P(("ctx", "head"), None),
            P(("ctx", "head"), None),
            P(("ctx", "head"), None),
            P(("ctx", "head"), None),
            P(),
            P(),
            P(),
        ),
        out_specs=(P("ctx", "head"), P("ctx", "head"), P("ctx", "head"), P("ctx", "head")),
        check_vma=False,
    )
```

profile of v0, /device:TPU:1, one launch (start us, length us, event | category | flops | bytes accessed | tf_op | source)
XLA Modules:
  0.0 378.2 jit_solution(5950468051867797090)
XLA Ops:
  8.1 16.7 %all_to_all.70 = bf16[64,8,128]{2,0,1:T(8,128)(2,1)} all-to-all(bf16[64,8,128]{2,0,1:T(8,128)(2,1)S(1)} %copy_bitcast_fusion.4), channel_id=1, replica_groups=mesh['ctx'=32,'head'=8] {'head'}, dimensions={1} | all-to-all | bytes 262144 | tf_op jit(solution)/shard_map/all_to_all | solution.py:27
  25.8 11.1 %all_to_all.71 = bf16[64,8,128]{2,0,1:T(8,128)(2,1)} all-to-all(bf16[64,8,128]{2,0,1:T(8,128)(2,1)S(1)} %copy_bitcast_fusion.3), channel_id=1, replica_groups=mesh['ctx'=32,'head'=8] {'head'}, dimensions={1} | all-to-all | bytes 262144 | tf_op jit(solution)/shard_map/all_to_all | solution.py:28
  36.9 1.9 copy.91
  38.8 3.5 all-to-all-start.1
  44.0 1.9 copy.90
  46.0 10.4 %all-to-all-done.1 = bf16[64,8,512]{2,0,1:T(8,128)(2,1)S(1)} async-done(((bf16[64,8,512]{2,0,1:T(8,128)(2,1)}), bf16[64,8,512]{2,0,1:T(8,128)(2,1)S(1)}, u32[]{:S(2)}, u32[]{:S(2)}) %all-to-all-start.1) | async-done | bytes 524320 | tf_op jit(solution)/shard_map/all_to_all | solution.py:26
  56.4 3.5 all-to-all-start.3
  62.2 2.0 sort.17
  64.9 7.0 %all-to-all-done.3 = bf16[64,8,512]{2,0,1:T(8,128)(2,1)S(1)} async-done(((bf16[64,8,512]{2,0,1:T(8,128)(2,1)}), bf16[64,8,512]{2,0,1:T(8,128)(2,1)S(1)}, u32[]{:S(2)}, u32[]{:S(2)}) %all-to-all-start.3) | async-done | bytes 524320 | tf_op jit(solution)/shard_map/all_to_all | solution.py:29
  74.6 53.1 %all-gather.5.cloned.1.call-done = bf16[16384,128]{1,0:T(8,128)(2,1)} async-done(((bf16[512,128]{1,0:T(8,128)(2,1)}), bf16[16384,128]{1,0:T(8,128)(2,1)}) %all-gather.5.cloned.1.call-update) | async-done | bytes 4194320 | tf_op jit(solution)/shard_map/all_gather | solution.py:57
  127.8 39.1 %while.30 = (s32[]{:T(128)}, f32[1,4,512]{2,1,0:T(4,128)S(1)}, f32[1,4,512]{2,1,0:T(4,128)S(1)}, f32[1,4,512,128]{3,2,1,0:T(8,128)S(1)}, s32[]{:T(128)}, /*index...) while((s32[]{:T(128)}, f32[1,4,512]{2,1,0:T(4,128)S(1)}, ...), condition=%wide.region_9.10_spmd, body=%wide.region_6.9_spmd.sunk | while | flops 551053824 | bytes 17219468 | solution.py:114
  136.0 1.5 fusion.120
  145.8 1.5 fusion.120
  155.6 1.5 fusion.120
  165.3 1.5 fusion.120
  168.4 7.7 %broadcast_in_dim.106 = f32[16384,256]{0,1:T(8,128)} broadcast(f32[]{:T(128)} %constant.173.clone.1), dimensions={} | broadcast | bytes 16777220 | tf_op jit(solution)/shard_map/broadcast_in_dim | solution.py:165
  176.1 57.9 %while.31 = (s32[]{:T(128)}, f32[512,1,4,128]{0,3,2,1:T(8,128)S(1)}, f32[16384,256]{0,1:T(8,128)}, s32[]{:T(128)}, s32[66]{0:T(128)S(1)}, /*index=5*/bf16[16384,...) while((s32[]{:T(128)}, ...), condition=%wide.region_11.12_spmd, body=%wide.region_10.11_spmd.sunk | while | flops 1355620864 | bytes 27451300 | solution.py:167
  184.3 1.5 fusion.132
  187.1 1.7 fusion.136
  188.9 1.7 fusion.137
  198.8 1.5 fusion.132
  201.6 1.7 fusion.136
  203.4 1.7 fusion.137
  213.3 1.5 fusion.132
  216.1 1.7 fusion.136
  217.8 1.7 fusion.137
  227.8 1.5 fusion.132
  230.6 1.7 fusion.136
  232.3 1.7 fusion.137
  234.0 13.8 %copy.59 = bf16[16384,256]{1,0:T(8,128)(2,1)} copy(f32[16384,256]{0,1:T(8,128)} %get-tuple-element.415) | data formatting | bytes 25165824 | tf_op jit(solution)/shard_map/while | solution.py:167
  250.2 119.7 %reduce-scatter.2.cloned.1.call-done = bf16[512,256]{1,0:T(8,128)(2,1)} async-done(((bf16[16384,256]{1,0:T(8,128)(2,1)}), bf16[512,256]{1,0:T(8,128)(2,1)}) %reduce-scatter.2.cloned.1.call-update) | async-done | bytes 262160 | tf_op jit(solution)/shard_map/reduce_scatter | solution.py:168
  370.0 1.7 fusion.83
  (180 shorter events, 72.6 us)
Async XLA Ops:
  7.2 0.9 copy-start
  7.2 38.7 %copy-start.2 = (s32[64]{0:T(128)S(1)}, s32[64]{0:T(128)}, u32[]{:S(2)}) copy-start(s32[64]{0:T(128)} %param.17) | copy-start | bytes 772
  7.2 54.0 %copy-start.3 = (s32[13]{0:T(128)S(1)}, s32[13]{0:T(128)}, u32[]{:S(2)}) copy-start(s32[13]{0:T(128)} %param.15) | copy-start | bytes 160
  7.2 67.4 %all-gather.3.cloned.1.call-start = ((), (), s32[]{:S(2)}) async-start(), calls=%async_computation.5 | async-start | bytes 4325376 | tf_op jit(solution)/shard_map/all_gather | solution.py:56
  24.8 102.9 %all-gather.5.cloned.1.call-start = ((), (), s32[]{:S(2)}) async-start(), calls=%async_computation.6 | async-start | bytes 4325376 | tf_op jit(solution)/shard_map/all_gather | solution.py:57
  38.8 17.6 %all-to-all-start.1 = ((bf16[64,8,512]{2,0,1:T(8,128)(2,1)}), bf16[64,8,512]{2,0,1:T(8,128)(2,1)S(1)}, u32[]{:S(2)}, u32[]{:S(2)}) async-start(bf16[64,8,512]{2,0,1:T(8,128)(2,1)} %bitcast.184), calls=%async_computation.1 | async-start | bytes 1048576 | tf_op jit(solution)/shard_map/all_to_all | solution.py:26
  56.4 15.5 %all-to-all-start.3 = ((bf16[64,8,512]{2,0,1:T(8,128)(2,1)}), bf16[64,8,512]{2,0,1:T(8,128)(2,1)S(1)}, u32[]{:S(2)}, u32[]{:S(2)}) async-start(bf16[64,8,512]{2,0,1:T(8,128)(2,1)} %bitcast.183), calls=%async_computation.3 | async-start | bytes 1048576 | tf_op jit(solution)/shard_map/all_to_all | solution.py:29
  59.9 310.1 %reduce-scatter.2.cloned.1.call-start = ((), (), s32[]{:S(2)}) async-start(), calls=%async_computation.7 | async-start | bytes 8650752 | tf_op jit(solution)/shard_map/reduce_scatter | solution.py:168
  168.4 7.7 %copy-start.1 = (bf16[512,1,4,128]{0,3,2,1:T(8,128)(2,1)S(1)}, bf16[512,1,4,128]{0,3,2,1:T(8,128)(2,1)}, u32[]{:S(2)}) copy-start(bf16[512,1,4,128]{0,3,2,1:T(8,128)(2,1)} %copy.57) | copy-start | bytes 1572868
Sparse Core Ops, SparseCore 0:
  24.9 49.6 all-gather.2
  77.2 50.4 all-gather.4
  247.9 121.9 reduce-scatter.1
where the time goes:
time: 381 us; the launch traced here: 378 us
  waiting for transfers between devices  192 us (50%)
  local copies, waits for them, and re-layouts  63.7 us (17%)
  other arithmetic  33.3 us (9%)
  matrix products  28.7 us (8%)
  blocking collectives  27.8 us (7%)
  between operations  14.6 us (4%)
  loops' own time  11.3 us (3%)
  starting transfers between devices  7.11 us (2%)
    reduce_scatter x1, waiting for transfers between devices, on_device(): lax.psum_scatter(partials.astype(jnp.bfloat16), 'ctx', scatter_dimension=...  120 us
    all_gather x1, waiting for transfers between devices, on_device(): lax.all_gather(my_values, 'ctx', axis=0, tiled=True)  53.1 us
    all_to_all x1, blocking collectives, on_device(): lax.all_to_all(key_states, 'head', split_axis=1, concat_axis=0, tiled=True)  16.7 us
    while x3, local copies, waits for them, and re-layouts, on_device(): query_sum, partials = lax.fori_loop(0, turn_count, joint_step, start_joint)  15.3 us
    dynamic_update_slice x8, other arithmetic, joint_step(): lax.dynamic_update_slice_in_dim(partials, current + joined[slot_index * B...  13.6 us
    all_to_all x1, blocking collectives, on_device(): lax.all_to_all(value_states, 'head', split_axis=1, concat_axis=0, tiled=T...  11.1 us
    all_to_all x1, waiting for transfers between devices, on_device(): lax.all_to_all(queries, 'head', split_axis=1, concat_axis=0, tiled=True)  10.4 us
    dynamic_slice x8, local copies, waits for them, and re-layouts, key_group(): value_parts.append(lax.dynamic_slice_in_dim(all_values, first_row, BLOCK))  7.7 us
  transfers between devices with their start and end apart: 5, of which 5 were waited for; matrix products, arithmetic and copies ran while one was open for 4% of the time, Pallas kernels for 0%

commit v1 on v0

v1 whole, which is shorter than its diff:
```python
import functools

import jax
import jax.numpy as jnp
from jax import lax
from jax.experimental import pallas as pl
from jax.experimental.pallas import tpu as pltpu
from jax.sharding import PartitionSpec as P

HD = 128
BLOCK = 256
SPAN = 7
MESH = pl.DeviceIdType.MESH
LOG2E = 1.4426950408889634


def greet(ctx_count, head_count, ctx_me, head_me, with_heads):
    barrier = pltpu.get_barrier_semaphore()

    def greet_ctx(r, carry):
        pl.semaphore_signal(
            barrier, inc=1, device_id=(lax.rem(ctx_me + r, ctx_count), head_me), device_id_type=MESH
        )
        return carry

    lax.fori_loop(1, ctx_count, greet_ctx, 0)
    total = ctx_count - 1
    if with_heads:

        def greet_head(r, carry):
            pl.semaphore_signal(
                barrier,
                inc=1,
                device_id=(ctx_me, lax.rem(head_me + r, head_count)),
                device_id_type=MESH,
            )
            return carry

        lax.fori_loop(1, head_count, greet_head, 0)
        total += head_count - 1
    pl.semaphore_wait(barrier, total)


def drain(ref, sem):
    pltpu.make_async_copy(ref, ref, sem).wait()


def spread_kernel(
    ctx_count,
    head_count,
    slots,
    list_ref,
    q_ref,
    k_ref,
    v_ref,
    g_ref,
    q_out,
    g_out,
    kv_out,
    landed,
    pieces,
    staged,
    kv_send,
    kv_recv,
    wide_send,
    wide_recv,
    piece_send,
    piece_recv,
    list_send,
    list_recv,
):
    ctx_me = lax.axis_index("ctx")
    head_me = lax.axis_index("head")
    rows = k_ref.shape[0]
    wide = q_ref.shape[1] // head_count
    part_rows = pieces.shape[1]
    greet(ctx_count, head_count, ctx_me, head_me, True)

    my_rows = pl.ds(pl.multiple_of(head_me * rows, rows), rows)
    for which, ref in enumerate((k_ref, v_ref)):

        def send_narrow(r, carry, which=which, ref=ref):
            peer = lax.rem(head_me + r, head_count)
            pltpu.make_async_remote_copy(
                src_ref=ref.at[:, pl.ds(pl.multiple_of(peer * HD, HD), HD)],
                dst_ref=landed.at[which, my_rows],
                send_sem=kv_send,
                recv_sem=kv_recv,
                device_id=(ctx_me, peer),
                device_id_type=MESH,
            ).start()
            return carry

        lax.fori_loop(1, head_count, send_narrow, 0)
        pltpu.make_async_copy(
            ref.at[:, pl.ds(pl.multiple_of(head_me * HD, HD), HD)],
            landed.at[which, my_rows],
            kv_recv,
        ).start()
    for which, (ref, out) in enumerate(((q_ref, q_out), (g_ref, g_out))):

        def send_wide(r, carry, ref=ref, out=out, which=which):
            peer = lax.rem(head_me + r, head_count)
            pltpu.make_async_remote_copy(
                src_ref=ref.at[:, pl.ds(pl.multiple_of(peer * wide, wide), wide)],
                dst_ref=out.at[my_rows],
                send_sem=wide_send.at[which],
                recv_sem=wide_recv.at[which],
                device_id=(ctx_me, peer),
                device_id_type=MESH,
            ).start()
            return carry

        lax.fori_loop(1, head_count, send_wide, 0)
        pltpu.make_async_copy(
            ref.at[:, pl.ds(pl.multiple_of(head_me * wide, wide), wide)],
            out.at[my_rows],
            wide_recv.at[which],
        ).start()

    drain(landed, kv_recv)
    blocks = landed.shape[1] // BLOCK
    my_blocks = pl.ds(ctx_me * blocks, blocks)
    my_kind = lax.rem(ctx_me, 2)
    my_part = lax.div(ctx_me, 2)

    def piece_of(device, block):
        start = pl.multiple_of(block * BLOCK + lax.div(device, 2) * part_rows, part_rows)
        return landed.at[lax.rem(device, 2), pl.ds(start, part_rows)]

    for block in range(blocks):

        def send_piece(r, carry, block=block):
            peer = lax.rem(ctx_me + r, ctx_count)
            pltpu.make_async_remote_copy(
                src_ref=piece_of(peer, block),
                dst_ref=pieces.at[ctx_me * blocks + block],
                send_sem=piece_send,
                recv_sem=piece_recv,
                device_id=(peer, head_me),
                device_id_type=MESH,
            ).start()
            return carry

        lax.fori_loop(1, ctx_count, send_piece, 0)
        pltpu.make_async_copy(
            piece_of(ctx_me, block), pieces.at[ctx_me * blocks + block], piece_recv
        ).start()
    drain(pieces, piece_recv)

    my_part_rows = pl.ds(pl.multiple_of(my_part * part_rows, part_rows), part_rows)

    def stage(peer):
        for slot in range(slots):
            staged[peer, slot] = pieces[list_ref[peer * slots + slot]]

    def send_listed(r, carry):
        peer = lax.rem(ctx_me + r, ctx_count)
        stage(peer)
        pltpu.make_async_remote_copy(
            src_ref=staged.at[peer],
            dst_ref=kv_out.at[my_kind, :, my_part_rows],
            send_sem=list_send,
            recv_sem=list_recv,
            device_id=(peer, head_me),
            device_id_type=MESH,
        ).start()
        return carry

    lax.fori_loop(1, ctx_count, send_listed, 0)
    stage(ctx_me)
    pltpu.make_async_copy(
        staged.at[ctx_me], kv_out.at[my_kind, :, my_part_rows], list_recv
    ).start()

    drain(kv_out, list_recv)
    drain(q_out, wide_recv.at[0])
    drain(g_out, wide_recv.at[1])
    sent = rows * (head_count - 1)
    drain(landed.at[0, pl.ds(0, sent)], kv_send)
    drain(landed.at[1, pl.ds(0, sent)], kv_send)
    drain(q_out.at[pl.ds(0, sent)], wide_send.at[0])
    drain(g_out.at[pl.ds(0, sent)], wide_send.at[1])
    drain(pieces.at[pl.ds(0, (ctx_count - 1) * blocks)], piece_send)
    drain(staged.at[pl.ds(0, ctx_count - 1)], list_send)


def gather_kernel(
    ctx_count,
    slots,
    table_ref,
    part_ref,
    out_ref,
    arrived,
    summed,
    part_send,
    part_recv,
    sum_send,
    sum_recv,
):
    ctx_me = lax.axis_index("ctx")
    head_me = lax.axis_index("head")
    part_rows = arrived.shape[1]
    blocks = summed.shape[1]
    greet(ctx_count, 1, ctx_me, head_me, False)
    my_slots = pl.ds(ctx_me * slots, slots)

    def rows_of(device):
        return pl.ds(pl.multiple_of(lax.div(device, 2) * part_rows, part_rows), part_rows)

    def send_part(r, carry):
        peer = lax.rem(ctx_me + r, ctx_count)
        pltpu.make_async_remote_copy(
            src_ref=part_ref.at[lax.rem(peer, 2), :, rows_of(peer)],
            dst_ref=arrived.at[my_slots],
            send_sem=part_send,
            recv_sem=part_recv,
            device_id=(peer, head_me),
            device_id_type=MESH,
        ).start()
        return carry

    lax.fori_loop(1, ctx_count, send_part, 0)
    pltpu.make_async_copy(
        part_ref.at[lax.rem(ctx_me, 2), :, rows_of(ctx_me)], arrived.at[my_slots], part_recv
    ).start()
    arrived[ctx_count * slots] = jnp.zeros(arrived.shape[1:], arrived.dtype)
    every = arrived.at[pl.ds(0, ctx_count * slots)]
    drain(every, part_recv)

    def add_up(peer):
        for block in range(blocks):
            first = (peer * blocks + block) * SPAN
            total = arrived[table_ref[first]].astype(jnp.float32)
            for step in range(1, SPAN):
                total = total + arrived[table_ref[first + step]].astype(jnp.float32)
            summed[peer, block] = total.astype(summed.dtype)

    def send_sum(r, carry):
        peer = lax.rem(ctx_me + r, ctx_count)
        add_up(peer)
        pltpu.make_async_remote_copy(
            src_ref=summed.at[peer],
            dst_ref=out_ref.at[lax.rem(ctx_me, 2), :, rows_of(ctx_me)],
            send_sem=sum_send,
            recv_sem=sum_recv,
            device_id=(peer, head_me),
            device_id_type=MESH,
        ).start()
        return carry

    lax.fori_loop(1, ctx_count, send_sum, 0)
    add_up(ctx_me)
    pltpu.make_async_copy(
        summed.at[ctx_me], out_ref.at[lax.rem(ctx_me, 2), :, rows_of(ctx_me)], sum_recv
    ).start()
    drain(out_ref, sum_recv)
    drain(arrived.at[pl.ds(0, (ctx_count - 1) * slots)], part_send)
    drain(summed.at[pl.ds(0, ctx_count - 1)], sum_send)


def attend_kernel(
    docs,
    group,
    meta_ref,
    q_ref,
    g_ref,
    kv_ref,
    o_ref,
    dq_ref,
    part_ref,
    scores,
    offset,
    maxima,
    totals,
    running,
    delta,
):
    scale = HD**-0.5
    exp_scale = scale * LOG2E
    rows_last = lax.broadcasted_iota(jnp.int32, (BLOCK, BLOCK), 0)
    cols_last = lax.broadcasted_iota(jnp.int32, (BLOCK, BLOCK), 1)
    contract_last = (((1,), (1,)), ((), ()))
    contract_first = (((0,), (0,)), ((), ()))

    def twice(ref):
        half = ref[...]
        return jnp.concatenate([half, half], axis=1)

    def query_block(index, carry):
        block = meta_ref[index]
        count = meta_ref[2 + index]
        base = index * meta_ref[2]
        rows = pl.ds(pl.multiple_of(index * BLOCK, BLOCK), BLOCK)
        q_pos = rows_last + block * BLOCK
        first = jnp.zeros((BLOCK, BLOCK), jnp.int32)
        for doc in range(docs - 1):
            end = meta_ref[4 + doc]
            first = jnp.where(q_pos >= end, end, first)
        offset[...] = cols_last - first
        maxima[...] = jnp.full_like(maxima, -jnp.inf)
        totals[...] = jnp.zeros_like(totals)
        running[...] = jnp.zeros_like(running)

        def score_step(turn, carry):
            keys = kv_ref[0, base + turn]
            allowed = (offset[...] >= (turn - block) * BLOCK) & (
                cols_last - rows_last <= turn * BLOCK
            )
            bias = jnp.where(allowed, 0.0, -jnp.inf)
            for g in range(group):
                tile = lax.dot_general(
                    q_ref[rows, g * HD : (g + 1) * HD],
                    keys,
                    contract_last,
                    preferred_element_type=jnp.float32,
                )
                tile = tile + bias
                scores[turn, g] = tile
                maxima[g] = jnp.maximum(
                    maxima[g], jnp.maximum(tile[:, :HD], tile[:, HD:])
                )
            return carry

        lax.fori_loop(0, count, score_step, 0)
        for g in range(group):
            top = jnp.max(maxima[g], axis=1, keepdims=True) * exp_scale
            maxima[g] = jnp.broadcast_to(top, (BLOCK, HD))

        def weight_step(turn, carry):
            values = kv_ref[1, base + turn]
            for g in range(group):
                tile = jnp.exp2(scores[turn, g] * exp_scale - twice(maxima.at[g]))
                scores[turn, g] = tile
                totals[g] = totals[g] + (tile[:, :HD] + tile[:, HD:])
                running[g] = running[g] + jnp.dot(
                    tile.astype(jnp.bfloat16), values, preferred_element_type=jnp.float32
                )
            return carry

        lax.fori_loop(0, count, weight_step, 0)
        for g in range(group):
            columns = slice(g * HD, (g + 1) * HD)
            inverse = 1.0 / jnp.sum(totals[g], axis=1, keepdims=True)
            totals[g] = jnp.broadcast_to(inverse, (BLOCK, HD))
            result = (running[g] * totals[g]).astype(jnp.bfloat16)
            o_ref[rows, columns] = result
            product = result.astype(jnp.float32) * g_ref[rows, columns].astype(jnp.float32)
            delta[g] = jnp.broadcast_to(
                jnp.sum(product, axis=1, keepdims=True), (BLOCK, HD)
            )
        running[...] = jnp.zeros_like(running)

        def grad_step(turn, carry):
            keys = kv_ref[0, base + turn]
            values = kv_ref[1, base + turn]
            key_grad = jnp.zeros((BLOCK, HD), jnp.float32)
            value_grad = jnp.zeros((BLOCK, HD), jnp.float32)
            for g in range(group):
                columns = slice(g * HD, (g + 1) * HD)
                out_grad = g_ref[rows, columns]
                weights = scores[turn, g] * twice(totals.at[g])
                prob_grad = lax.dot_general(
                    out_grad, values, contract_last, preferred_element_type=jnp.float32
                )
                score_grad = (weights * (prob_grad - twice(delta.at[g]))).astype(jnp.bfloat16)
                running[g] = running[g] + jnp.dot(
                    score_grad, keys, preferred_element_type=jnp.float32
                )
                key_grad = key_grad + lax.dot_general(
                    score_grad,
                    q_ref[rows, columns],
                    contract_first,
                    preferred_element_type=jnp.float32,
                )
                value_grad = value_grad + lax.dot_general(
                    weights.astype(jnp.bfloat16),
                    out_grad,
                    contract_first,
                    preferred_element_type=jnp.float32,
                )
            part_ref[0, base + turn] = (key_grad * scale).astype(jnp.bfloat16)
            part_ref[1, base + turn] = value_grad.astype(jnp.bfloat16)
            return carry

        lax.fori_loop(0, count, grad_step, 0)
        for g in range(group):
            dq_ref[rows, g * HD : (g + 1) * HD] = (running[g] * scale).astype(jnp.bfloat16)
        return carry

    lax.fori_loop(0, 2, query_block, 0)


def spread(slots, ids, ctx_count, head_count, listing, queries, keys, values, grads):
    rows = queries.shape[0] * head_count
    wide = queries.shape[1] // head_count
    blocks = rows // BLOCK
    part_rows = 2 * BLOCK // ctx_count
    anywhere = pl.BlockSpec(memory_space=pl.ANY)
    bf16 = jnp.bfloat16
    return pl.pallas_call(
        functools.partial(spread_kernel, ctx_count, head_count, slots),
        out_shape=(
            jax.ShapeDtypeStruct((rows, wide), bf16),
            jax.ShapeDtypeStruct((rows, wide), bf16),
            jax.ShapeDtypeStruct((2, slots, BLOCK, HD), bf16),
        ),
        in_specs=[pl.BlockSpec(memory_space=pltpu.SMEM)] + [anywhere] * 4,
        out_specs=[anywhere] * 3,
        scratch_shapes=[
            pltpu.VMEM((2, rows, HD), bf16),
            pltpu.VMEM((ctx_count * blocks, part_rows, HD), bf16),
            pltpu.VMEM((ctx_count, slots, part_rows, HD), bf16),
            pltpu.SemaphoreType.DMA,
            pltpu.SemaphoreType.DMA,
            pltpu.SemaphoreType.DMA((2,)),
            pltpu.SemaphoreType.DMA((2,)),
            pltpu.SemaphoreType.DMA,
            pltpu.SemaphoreType.DMA,
            pltpu.SemaphoreType.DMA,
            pltpu.SemaphoreType.DMA,
        ],
        compiler_params=pltpu.CompilerParams(
            collective_id=ids, has_side_effects=True, vmem_limit_bytes=48 << 20
        ),
        name="spread",
    )(listing, queries, keys, values, grads)


def attend(slots, docs, meta, queries, grads, kv):
    rows, wide = queries.shape
    group = wide // HD
    whole = pl.BlockSpec(memory_space=pltpu.VMEM)
    stat = pltpu.VMEM((group, BLOCK, HD), jnp.float32)
    return pl.pallas_call(
        functools.partial(attend_kernel, docs, group),
        out_shape=(
            jax.ShapeDtypeStruct((rows, wide), jnp.bfloat16),
            jax.ShapeDtypeStruct((rows, wide), jnp.bfloat16),
            jax.ShapeDtypeStruct(kv.shape, jnp.bfloat16),
        ),
        in_specs=[pl.BlockSpec(memory_space=pltpu.SMEM)] + [whole] * 3,
        out_specs=[whole] * 3,
        scratch_shapes=[
            pltpu.VMEM((SPAN, group, BLOCK, BLOCK), jnp.float32),
            pltpu.VMEM((BLOCK, BLOCK), jnp.int32),
            stat,
            stat,
            stat,
            stat,
        ],
        compiler_params=pltpu.CompilerParams(vmem_limit_bytes=48 << 20),
        name="attend",
    )(meta, queries, grads, kv)


def gather(slots, ids, ctx_count, table, part):
    blocks = 2
    part_rows = 2 * BLOCK // ctx_count
    anywhere = pl.BlockSpec(memory_space=pl.ANY)
    bf16 = jnp.bfloat16
    return pl.pallas_call(
        functools.partial(gather_kernel, ctx_count, slots),
        out_shape=jax.ShapeDtypeStruct((2, blocks, BLOCK, HD), bf16),
        in_specs=[pl.BlockSpec(memory_space=pltpu.SMEM), anywhere],
        out_specs=anywhere,
        scratch_shapes=[
            pltpu.VMEM((ctx_count * slots + 1, part_rows, HD), bf16),
            pltpu.VMEM((ctx_count, blocks, part_rows, HD), bf16),
            pltpu.SemaphoreType.DMA,
            pltpu.SemaphoreType.DMA,
            pltpu.SemaphoreType.DMA,
            pltpu.SemaphoreType.DMA,
        ],
        compiler_params=pltpu.CompilerParams(
            collective_id=ids, has_side_effects=True, vmem_limit_bytes=48 << 20
        ),
        name="gather",
    )(table, part)


def on_device(ctx_count, head_count, queries, keys, values, grads, lengths, key_first, order):
    block_count = order.shape[0]
    docs = lengths.shape[0]
    ids = jnp.arange(block_count, dtype=jnp.int32)
    match = order[None, :] == ids[:, None]
    inverse = jnp.sum(jnp.where(match, ids[None, :], 0), axis=1)
    first = jnp.sum(jnp.where(match, key_first[:, None], 0), axis=0)
    counts = order - first + 1
    pair_order = order.reshape(ctx_count, 2)
    pair_counts = counts.reshape(ctx_count, 2)
    most = jnp.max(jnp.sum(pair_counts, axis=1))
    ctx_me = lax.axis_index("ctx")
    meta = jnp.concatenate(
        [
            lax.dynamic_index_in_dim(pair_order, ctx_me, 0, False),
            lax.dynamic_index_in_dim(pair_counts, ctx_me, 0, False),
            jnp.cumsum(lengths),
        ]
    )

    def branch(slots, base_id, queries, keys, values, grads):
        turn = jnp.arange(slots, dtype=jnp.int32)[None, :]
        head = pair_counts[:, :1]
        wanted = jnp.where(turn < head, pair_order[:, :1] - turn, pair_order[:, 1:] - turn + head)
        listing = jnp.sum(
            jnp.where(wanted[:, :, None] == order[None, None, :], ids[None, None, :], 0), axis=2
        ).reshape(-1)
        ahead = jnp.arange(SPAN, dtype=jnp.int32)[None, :]
        reader = order[:, None] + ahead
        seen = (reader[:, :, None] == order[None, None, :]) & (
            first[None, None, :] <= order[:, None, None]
        )
        place = (ids // 2) * slots + jnp.where(
            ids % 2 == 1, jnp.repeat(pair_counts[:, 0], 2), 0
        )
        table = jnp.sum(
            jnp.where(seen, place[None, None, :] + ahead[:, :, None] - ctx_count * slots, 0), axis=2
        ) + ctx_count * slots
        my_q, my_g, kv = spread(
            slots, base_id, ctx_count, head_count, listing, queries, keys, values, grads
        )
        attended, query_grad, part = attend(slots, docs, meta, my_q, my_g, kv)
        total = gather(slots, base_id + 1, ctx_count, table.reshape(-1), part)
        rows = attended.shape[0]
        return attended, query_grad, total[0].reshape(rows, HD), total[1].reshape(rows, HD)

    return lax.cond(
        most <= 9,
        functools.partial(branch, 9, 0),
        functools.partial(branch, 2 * SPAN, 2),
        queries,
        keys,
        values,
        grads,
    )


def solution(mesh):
    return jax.shard_map(
        functools.partial(on_device, mesh.shape["ctx"], mesh.shape["head"]),
        mesh=mesh,
        in_specs=(
            P(("ctx", "head"), None),
            P(("ctx", "head"), None),
            P(("ctx", "head"), None),
            P(("ctx", "head"), None),
            P(),
            P(),
            P(),
        ),
        out_specs=(P("ctx", "head"), P("ctx", "head"), P("ctx", "head"), P("ctx", "head")),
        check_vma=False,
    )
```

time: 381 us -> 103 us (0.27)
  waiting for transfers between devices: 192 us -> 0 us
  Pallas kernels: 0 us -> 93.8 us
  local copies, waits for them, and re-layouts: 63.7 us -> 2.36 us
  other arithmetic: 33.3 us -> 4.57 us
  matrix products: 28.7 us -> 0 us
  blocking collectives: 27.8 us -> 0 us
  between operations: 14.6 us -> 1.32 us
  loops' own time: 11.3 us -> 0.1 us
  starting transfers between devices: 7.11 us -> 0 us
    reduce_scatter x1 -> x0, waiting for transfers between devices: 120 us -> none  [on_device(): lax.psum_scatter(partials.astype(jnp.bfloat16), 'ctx', scatter_dimension=...]
    pallas_call x0 -> x3, Pallas kernels: none -> 93.8 us  [the longest x1 44.4 us: spread(): pl.pallas_call(functools.partial(spread_kernel, ctx_count, head_count, sl...]
    all_gather x2 -> x0, waiting for transfers between devices: 54.4 us -> none  [the longest x1 53.1 us: on_device(): lax.all_gather(my_values, 'ctx', axis=0, tiled=True)]
    dot_general x28 -> x0, matrix products: 28.7 us -> none  [the longest x8 6.2 us: tile_scores(): jnp.einsum('qhgd,khd->hgqk', query_tile, key_tile, preferred_element_type...]
    all_to_all x2 -> x0, blocking collectives: 27.8 us -> none  [the longest x1 16.7 us: on_device(): lax.all_to_all(key_states, 'head', split_axis=1, concat_axis=0, tiled=True)]
    all_to_all x2 -> x0, waiting for transfers between devices: 17.4 us -> none  [the longest x1 10.4 us: on_device(): lax.all_to_all(queries, 'head', split_axis=1, concat_axis=0, tiled=True)]
    while x8 -> x0, local copies, waits for them, and re-layouts: 15.3 us -> none  [the longest x3 15.3 us: on_device(): query_sum, partials = lax.fori_loop(0, turn_count, joint_step, start_joint)]
    dynamic_update_slice x8 -> x0, other arithmetic: 13.6 us -> none  [joint_step(): lax.dynamic_update_slice_in_dim(partials, current + joined[slot_index * B...]
  transfers between devices with their start and end apart: 5 -> 0, of which waited for: 5 -> 0; matrix products, arithmetic and copies ran while one was open for 4% -> 0% of each run, Pallas kernels for 0% -> 0%
where the time goes in v1:
time: 103 us; the launch traced here: 102 us
  Pallas kernels  93.8 us (91%)
  other arithmetic  4.57 us (4%)
  local copies, waits for them, and re-layouts  2.36 us (2%)
  between operations  1.32 us (1%)
    pallas_call x1, Pallas kernels, spread(): pl.pallas_call(functools.partial(spread_kernel, ctx_count, head_count, sl...  44.4 us
    pallas_call x1, Pallas kernels, gather(): pl.pallas_call(functools.partial(gather_kernel, ctx_count, slots), out_sh...  28.2 us
    pallas_call x1, Pallas kernels, attend(): pl.pallas_call(functools.partial(attend_kernel, docs, group), out_shape=(...  21.2 us

profile of v1, /device:TPU:1, one launch (start us, length us, event | category | flops | bytes accessed | tf_op | source)
XLA Modules:
  0.0 102.1 jit_solution(2680233595178027389)
XLA Ops:
  0.6 0.8 select_reduce_fusion.4
  1.4 0.7 subtract_add_fusion
  2.1 0.1 reshape.386
  2.2 0.8 reshape.387
  2.9 0.8 reduce-window.9
  3.8 0.1 pad_add_fusion
  3.9 0.1 reduce_sum.55
  4.0 0.6 reduce_max.9
  5.3 96.9 %conditional.1 = (bf16[512,512]{1,0:T(8,128)(2,1)}, bf16[512,512]{1,0:T(8,128)(2,1)}, bf16[512,128]{1,0:T(8,128)(2,1)}, bf16[512,128]{1,0:T(8,128)(2,1)}) conditional(s32[]{:T(128)} %convert_element_type.3, (s32[32,2]{1,0:T(8,128)S(1)}, s32[32,2]{1,0:T(8,128)S(1)}, s32[64]{0:T(128)}, s32[64]{0:T(128)S(1)}, bf16[64,4096]{1,0:T(8,128)(2,1)}, ...), branch_computations={%region_4.7_spmd, %region_7.10_spmd} | conditional | flops 209856 | bytes 571708 | solution.py:528
  5.3 0.1 copy.37
  5.4 0.1 copy.38
  5.5 0.0 copy-start.1
  5.5 1.1 %select_reduce_fusion.3 = s32[32,9]{0,1:T(8,128)S(1)} fusion(s32[64]{0:T(128)S(1)} %get-tuple-element.78, s32[64]{0:T(128)} %get-tuple-element.65, s32[32,9]{0,1:T(8,128)S(1)} %add_select_fusion.1), kind=kLoop, calls=%fused_computation.22 | loop fusion | flops 55008 | bytes 2816 | tf_op jit(solution)/shard_map/cond/branch_1_fun/reduce_sum | solution.py:506
  6.5 0.1 copy.33
  6.6 0.1 reshape.380.list_ref
  6.7 44.4 %spread.3 = (bf16[512,512]{1,0:T(8,128)(2,1)S(1)}, bf16[512,512]{1,0:T(8,128)(2,1)S(1)}, bf16[2,9,256,128]{3,2,1,0:T(8,128)(2,1)S(1)}) custom-call(s32[288]{0:T(512)S(1)} %reshape.380.list_ref, bf16[64,4096]{1,0:T(8,128)(2,1)} %get-tuple-element.95.q_ref, bf16[64,1024]{1,0:T(8,128)(2,1)} %get-tuple-element.97.k_ref, ...), custom_call_target="tpu_custom_call" | custom-call | tf_op jit(solution)/shard_map/cond/branch_1_fun/spread/pallas_call | solution.py:401
  51.2 21.2 %attend.3 = (bf16[512,512]{1,0:T(8,128)(2,1)}, bf16[512,512]{1,0:T(8,128)(2,1)}, bf16[2,9,256,128]{3,2,1,0:T(8,128)(2,1)S(1)}) custom-call(s32[17]{0:T(128)S(1)} %get-tuple-element.62.meta_ref, bf16[512,512]{1,0:T(8,128)(2,1)S(1)} %get-tuple-element.71.q_ref, bf16[512,512]{1,0:T(8,128)(2,1)S(1)} %get-tuple-element.72.g_ref, ...), custom_call_target="tpu_custom_call" | custom-call | tf_op jit(solution)/shard_map/cond/branch_1_fun/attend/pallas_call | solution.py:435
  72.4 0.1 broadcast_in_dim.71
  72.4 0.1 reshape.381
  72.6 0.0 copy-done.1
  72.6 0.1 broadcast_compare_fusion.1
  72.7 0.3 select_reduce_fusion.2
  73.0 0.1 copy.34
  73.1 0.1 add.139.table_ref
  73.2 28.2 %gather.3 = bf16[2,2,256,128]{3,2,1,0:T(8,128)(2,1)S(1)} custom-call(s32[448]{0:T(512)S(1)} %add.139.table_ref, bf16[2,9,256,128]{3,2,1,0:T(8,128)(2,1)S(1)} %get-tuple-element.79.part_ref), custom_call_target="tpu_custom_call" | custom-call | tf_op jit(solution)/shard_map/cond/branch_1_fun/gather/pallas_call | solution.py:462
  101.4 0.7 fusion.5
  (8 shorter events, 0.1 us)
Async XLA Ops:
  5.5 67.1 %copy-start.1 = (s32[64]{0:T(128)S(1)}, s32[64]{0:T(128)}, u32[]{:S(2)}) copy-start(s32[64]{0:T(128)} %get-tuple-element.65) | copy-start | bytes 772 | tf_op jit(solution)/shard_map/cond

commit v2 on v0

v2 whole, which is shorter than its diff:
```python
import functools

import jax
import jax.numpy as jnp
from jax import lax
from jax.experimental import pallas as pl
from jax.experimental.pallas import tpu as pltpu
from jax.sharding import PartitionSpec as P

HD = 128
BLOCK = 256
SPAN = 7
CTX = 32
HEADS = 8
GROUP = 4
ROWS = 64
PIECE = 16
MESH = pl.DeviceIdType.MESH
LOG2E = 1.4426950408889634
SCALE = HD**-0.5
LAST = (((1,), (1,)), ((), ()))
FIRST = (((0,), (0,)), ((), ()))


def drain(ref, sem):
    pltpu.make_async_copy(ref, ref, sem).wait()


def loop(count, body):
    def step(index, carry):
        body(index)
        return carry

    lax.fori_loop(0, count, step, 0)


def greet(me, head):
    barrier = pltpu.get_barrier_semaphore()
    chip = lax.div(me, 2)

    def signal(ctx, z):
        pl.semaphore_signal(barrier, inc=1, device_id=(ctx, z), device_id_type=MESH)

    loop(CTX - 1, lambda r: signal(lax.rem(me + r + 1, CTX), head))
    loop(HEADS - 1, lambda r: signal(me, lax.rem(head + r + 1, HEADS)))
    for half in range(2):
        source = half * 4 + lax.div(chip, 4)
        loop(CTX - 1, lambda r: signal(lax.rem(me + r + 1, CTX), source))

        @pl.when(source != head)
        def _():
            signal(me, source)

    apart = lax.rem(lax.div(chip, 4) + 4 - lax.rem(head, 4), 4)
    pl.semaphore_wait(barrier, CTX - 1 + HEADS - 1 + 2 * CTX - 1 + lax.div(apart + 3, 4))


def fused_kernel(
    slots,
    docs,
    order_ref,
    inverse_ref,
    first_ref,
    lengths_ref,
    q_ref,
    k_ref,
    v_ref,
    g_ref,
    o_ref,
    dq_ref,
    dk_ref,
    dv_ref,
    table,
    q_buf,
    g_buf,
    g_scaled,
    q_now,
    kv,
    pieces,
    staged,
    bias,
    scores,
    probs,
    grads,
    wide_keys,
    wide_values,
    maxima,
    totals,
    delta,
    sums,
    part,
    o_buf,
    dq_buf,
    arrived,
    summed,
    piece_send,
    piece_recv,
    wide_send,
    wide_recv,
    list_send,
    list_recv,
    out_sem,
    part_send,
    part_recv,
    sum_send,
    sum_recv,
):
    me = lax.axis_index("ctx")
    head = lax.axis_index("head")
    chip, kind = lax.div(me, 2), lax.rem(me, 2)
    greet(me, head)

    def remote(src, dst, send, recv, ctx, z):
        pltpu.make_async_remote_copy(
            src_ref=src,
            dst_ref=dst,
            send_sem=send,
            recv_sem=recv,
            device_id=(ctx, z),
            device_id_type=MESH,
        ).start()

    pair = lax.div(head, 4)
    for which, ref in enumerate((k_ref, v_ref)):
        for p in range(4):
            target = (lax.rem(head, 4) * 4 + p) * 2 + which
            slot = pieces.at[me * 2 + pair]

            def send_piece(r, ref=ref, p=p, target=target, slot=slot):
                z = lax.rem(head + r, HEADS)
                src = ref.at[pl.ds(p * PIECE, PIECE), pl.ds(pl.multiple_of(z * HD, HD), HD)]
                remote(src, slot, piece_send, piece_recv, target, z)

            loop(HEADS - 1, lambda r, f=send_piece: f(r + 1))

            @pl.when(target != me)
            def _(f=send_piece):
                f(0)

            @pl.when(target == me)
            def _(ref=ref, p=p, slot=slot):
                src = ref.at[pl.ds(p * PIECE, PIECE), pl.ds(pl.multiple_of(head * HD, HD), HD)]
                pltpu.make_async_copy(src, slot, piece_recv).start()

    my_rows = pl.ds(pl.multiple_of(lax.rem(head, 4) * ROWS, ROWS), ROWS)

    def columns(z, g):
        return pl.ds(pl.multiple_of(z * GROUP * HD + g * HD, HD), HD)

    def send_heads(which, ref, buf):
        for g in range(GROUP):

            def send_wide(r, g=g):
                z = lax.rem(head + r + 1, HEADS)
                remote(
                    ref.at[:, columns(z, g)],
                    buf.at[g, pair, my_rows],
                    wide_send.at[which],
                    wide_recv.at[which, g],
                    me,
                    z,
                )

            loop(HEADS - 1, send_wide)
            pltpu.make_async_copy(
                ref.at[:, columns(head, g)], buf.at[g, pair, my_rows], wide_recv.at[which, g]
            ).start()

    send_heads(0, q_ref, q_buf)
    send_heads(1, g_ref, g_buf)

    rows = lax.broadcasted_iota(jnp.int32, (BLOCK, BLOCK), 0)
    cols = lax.broadcasted_iota(jnp.int32, (BLOCK, BLOCK), 1)

    def pair_of(device):
        block_a, block_b = order_ref[2 * device], order_ref[2 * device + 1]
        return block_a, block_b, block_a - first_ref[block_a] + 1

    block_a, block_b, count_a = pair_of(me)
    count_b = block_b - first_ref[block_b] + 1

    def chosen(t):
        return (t >= count_a).astype(jnp.int32)

    def make_bias(t):
        late = t >= count_a
        block = jnp.where(late, block_b, block_a)
        back = jnp.where(late, t - count_a, t)
        reach = jnp.where(t < count_a + count_b, back * BLOCK, -2 * BLOCK)
        low = jnp.zeros((BLOCK, BLOCK), jnp.int32)
        end = 0
        for doc in range(docs - 1):
            end = end + lengths_ref[doc]
            low = jnp.where(rows + block * BLOCK >= end, end, low)
        allowed = (cols + (block - back) * BLOCK >= low) & (cols - rows <= reach)
        bias[t] = jnp.where(allowed, 0.0, -jnp.inf)

    def rows_of(device):
        return pl.ds(pl.multiple_of(lax.div(device, 2) * PIECE, PIECE), PIECE)

    def send_lists():
        def stage(peer):
            first_block, second_block, first_count = pair_of(peer)
            for slot in range(slots):
                wanted = jnp.where(
                    slot < first_count, first_block - slot, second_block - slot + first_count
                )
                staged[peer, slot] = pieces[inverse_ref[jnp.maximum(wanted, 0)]]

        def send_list(r):
            peer = lax.rem(me + r + 1, CTX)
            stage(peer)
            remote(
                staged.at[peer],
                kv.at[kind, :, rows_of(me)],
                list_send,
                list_recv.at[kind],
                peer,
                head,
            )

        loop(CTX - 1, send_list)
        stage(me)
        pltpu.make_async_copy(
            staged.at[me], kv.at[kind, :, rows_of(me)], list_recv.at[kind]
        ).start()

    drain(pieces, piece_recv)
    pl.when(kind == 0)(send_lists)
    loop(slots, make_bias)
    drain(kv.at[0], list_recv.at[0])
    pl.when(kind == 1)(send_lists)

    def flags(t):
        late = (t >= count_a).astype(jnp.float32)
        return 1.0 - late, late

    def widen(wide, which, t):
        at = pl.ds(pl.multiple_of(t * BLOCK, BLOCK), BLOCK)
        zeros = jnp.zeros((BLOCK, HD), jnp.bfloat16)
        for i, flag in enumerate((t < count_a, t >= count_a)):
            spot = slice(i * HD, (i + 1) * HD)
            wide[at, spot] = jnp.where(flag, kv[which, t], zeros)

    unroll = 3 if slots % 3 == 0 else 2

    def tiles(body):
        def several(index):
            for u in range(unroll):
                body(index * unroll + u)

        loop(slots // unroll, several)

    def twice(half):
        return jnp.concatenate([half, half], axis=1)

    def tile_cols(t):
        return pl.ds(pl.multiple_of(t * BLOCK, BLOCK), BLOCK)

    def send_out(buf, ref, g, which):
        for i in range(2):
            pltpu.make_async_copy(
                buf.at[g, i],
                ref.at[pl.ds(i * BLOCK, BLOCK), pl.ds(pl.multiple_of(g * HD, HD), HD)],
                out_sem.at[which],
            ).start()

    def forward(g):
        drain(q_buf.at[g], wide_recv.at[0, g])
        q_now[...] = q_buf[g]
        maxima[...] = jnp.full_like(maxima, -jnp.inf)
        totals[g] = jnp.zeros(totals.shape[1:], jnp.float32)

        def score(t):
            tile = lax.dot_general(
                q_now[chosen(t)], kv[0, t], LAST, preferred_element_type=jnp.float32
            )
            tile = tile + bias[t]
            scores[t] = tile
            half = jnp.maximum(tile[:, :HD], tile[:, HD:])
            for i in range(2):
                penalty = jnp.where(chosen(t) == i, 0.0, -jnp.inf)
                maxima[i] = jnp.maximum(maxima[i], half + penalty)

        tiles(score)
        for i in range(2):
            top = jnp.max(maxima[i], axis=1, keepdims=True) * (SCALE * LOG2E)
            maxima[i] = jnp.broadcast_to(top, (BLOCK, HD))

        def weigh(t):
            tile = jnp.exp2(scores[t] * (SCALE * LOG2E) - twice(maxima[chosen(t)]))
            probs[g, :, tile_cols(t)] = tile.astype(jnp.bfloat16)
            half = tile[:, :HD] + tile[:, HD:]
            for i, flag in enumerate(flags(t)):
                totals[g, i] = totals[g, i] + half * flag

        tiles(weigh)
        for i in range(2):
            totals[g, i] = jnp.broadcast_to(
                1.0 / jnp.sum(totals[g, i], axis=1, keepdims=True), (BLOCK, HD)
            )

    def attend(g):
        both = jnp.dot(probs[g], wide_values[...], preferred_element_type=jnp.float32)
        for i in range(2):
            o_buf[g, i] = (
                both[:, i * HD : (i + 1) * HD] * totals[g, i]
            ).astype(jnp.bfloat16)
        send_out(o_buf, o_ref, g, 0)

    def prepare(g):
        drain(g_buf.at[g], wide_recv.at[1, g])
        for i in range(2):
            out_grad = g_buf[g, i].astype(jnp.float32) * totals[g, i]
            g_scaled[i] = out_grad.astype(jnp.bfloat16)
            row_sum = jnp.sum(o_buf[g, i].astype(jnp.float32) * out_grad, axis=1, keepdims=True)
            delta[i] = jnp.broadcast_to(row_sum, (BLOCK, HD))

    def value_grad(g, store):
        def step(t):
            store(
                t,
                lax.dot_general(
                    probs[g, :, tile_cols(t)],
                    g_scaled[chosen(t)],
                    FIRST,
                    preferred_element_type=jnp.float32,
                ),
            )

        tiles(step)

    def key_grad(g, store):
        def step(t):
            prob_grad = lax.dot_general(
                g_scaled[chosen(t)], kv[1, t], LAST, preferred_element_type=jnp.float32
            )
            score_grad = (
                probs[g, :, tile_cols(t)].astype(jnp.float32)
                * (prob_grad - twice(delta[chosen(t)]))
            ).astype(jnp.bfloat16)
            grads[g, :, tile_cols(t)] = score_grad
            store(
                t,
                lax.dot_general(
                    score_grad, q_buf[g, chosen(t)], FIRST, preferred_element_type=jnp.float32
                ),
            )

        tiles(step)

    def query_grad(g):
        both = jnp.dot(grads[g], wide_keys[...], preferred_element_type=jnp.float32)
        for i in range(2):
            dq_buf[g, i] = (
                both[:, i * HD : (i + 1) * HD] * SCALE
            ).astype(jnp.bfloat16)
        send_out(dq_buf, dq_ref, g, 1)

    sums[...] = jnp.zeros_like(sums)

    def keep(which):
        def store(t, value):
            sums[which, t] = sums[which, t] + value

        return store

    def finish(which, factor):
        def store(t, value):
            part[which, t] = ((sums[which, t] + value) * factor).astype(jnp.bfloat16)

        return store

    def send_parts(which):
        def send_part(peer_chip, core):
            peer = peer_chip * 2 + core
            remote(
                part.at[which, :, rows_of(peer)],
                arrived.at[pl.ds(me * slots, slots)],
                part_send,
                part_recv,
                peer,
                head,
            )

        loop(15, lambda r: send_part(lax.rem(chip + r + 1, 16), which))

        @pl.when(kind != which)
        def _():
            send_part(chip, which)

        @pl.when(kind == which)
        def _():
            pltpu.make_async_copy(
                part.at[which, :, rows_of(me)], arrived.at[pl.ds(me * slots, slots)], part_recv
            ).start()

    loop(slots, functools.partial(widen, wide_keys, 0))
    loop(GROUP, forward)
    drain(kv.at[1], list_recv.at[1])
    loop(slots, functools.partial(widen, wide_values, 1))
    loop(GROUP, attend)

    def one_head(g):
        prepare(g)
        value_grad(g, keep(1))
        key_grad(g, keep(0))

    loop(GROUP - 1, one_head)
    prepare(GROUP - 1)
    value_grad(GROUP - 1, finish(1, 1.0))
    send_parts(1)
    key_grad(GROUP - 1, finish(0, SCALE))
    send_parts(0)
    loop(GROUP, query_grad)

    nowhere = CTX * slots

    def make_table(place):
        block = order_ref[place]
        for step in range(SPAN):
            query = jnp.minimum(block + step, 2 * CTX - 1)
            spot = inverse_ref[query]
            device = lax.div(spot, 2)
            ahead = jnp.where(lax.rem(spot, 2) == 1, pair_of(device)[2], 0)
            listed = (block + step == query) & (first_ref[query] <= block)
            table[place * SPAN + step] = jnp.where(listed, device * slots + ahead + step, nowhere)

    loop(2 * CTX, make_table)
    arrived[nowhere] = jnp.zeros(arrived.shape[1:], arrived.dtype)
    drain(arrived.at[pl.ds(0, nowhere)], part_recv)

    def add_up(peer):
        for block in range(2):
            first = (peer * 2 + block) * SPAN
            total = arrived[table[first]].astype(jnp.float32)
            for step in range(1, SPAN):
                total = total + arrived[table[first + step]].astype(jnp.float32)
            summed[peer, block] = total.astype(summed.dtype)

    def send_sums(out_ref):
        def send_sum(r):
            peer = lax.rem(me + r + 1, CTX)
            add_up(peer)
            remote(
                summed.at[peer],
                out_ref.at[:, rows_of(me)],
                sum_send,
                sum_recv.at[kind],
                peer,
                head,
            )

        loop(CTX - 1, send_sum)
        add_up(me)
        pltpu.make_async_copy(
            summed.at[me], out_ref.at[:, rows_of(me)], sum_recv.at[kind]
        ).start()

    pl.when(kind == 0)(lambda: send_sums(dk_ref))
    pl.when(kind == 1)(lambda: send_sums(dv_ref))

    drain(pieces.at[pl.ds(0, ROWS - 1)], piece_send)

    @pl.when(lax.div(chip, 4) != lax.rem(head, 4))
    def _():
        drain(pieces.at[0], piece_send)

    for buf, which in ((q_buf, 0), (g_buf, 1)):
        for g in range(GROUP):
            drain(buf.at[g, 0], wide_send.at[which])
            drain(buf.at[g, 1, pl.ds(0, 3 * ROWS)], wide_send.at[which])
    drain(staged.at[pl.ds(0, CTX - 1)], list_send)
    drain(arrived.at[pl.ds(0, (CTX - 1) * slots)], part_send)
    drain(summed.at[pl.ds(0, CTX - 1)], sum_send)
    drain(o_buf, out_sem.at[0])
    drain(dq_buf, out_sem.at[1])
    drain(dk_ref, sum_recv.at[0])
    drain(dv_ref, sum_recv.at[1])


def fused(slots, identity, scalars, queries, keys, values, grads):
    docs = scalars[-1].shape[0]
    anywhere = pl.BlockSpec(memory_space=pl.ANY)
    small = pl.BlockSpec(memory_space=pltpu.SMEM)
    bf16, f32 = jnp.bfloat16, jnp.float32
    rows, wide = ROWS * HEADS, GROUP * HD
    dma = pltpu.SemaphoreType.DMA
    return pl.pallas_call(
        functools.partial(fused_kernel, slots, docs),
        out_shape=(
            jax.ShapeDtypeStruct((rows, wide), bf16),
            jax.ShapeDtypeStruct((rows, wide), bf16),
            jax.ShapeDtypeStruct((2, BLOCK, HD), bf16),
            jax.ShapeDtypeStruct((2, BLOCK, HD), bf16),
        ),
        in_specs=[small] * 4 + [anywhere] * 4,
        out_specs=[anywhere] * 4,
        scratch_shapes=[
            pltpu.SMEM((2 * CTX * SPAN,), jnp.int32),
            pltpu.VMEM((GROUP, 2, BLOCK, HD), bf16),
            pltpu.VMEM((GROUP, 2, BLOCK, HD), bf16),
            pltpu.VMEM((2, BLOCK, HD), bf16),
            pltpu.VMEM((2, BLOCK, HD), bf16),
            pltpu.VMEM((2, slots, BLOCK, HD), bf16),
            pltpu.VMEM((2 * CTX, PIECE, HD), bf16),
            pltpu.VMEM((CTX, slots, PIECE, HD), bf16),
            pltpu.VMEM((slots, BLOCK, BLOCK), f32),
            pltpu.VMEM((slots, BLOCK, BLOCK), f32),
            pltpu.VMEM((GROUP, BLOCK, slots * BLOCK), bf16),
            pltpu.VMEM((GROUP, BLOCK, slots * BLOCK), bf16),
            pltpu.VMEM((slots * BLOCK, 2 * HD), bf16),
            pltpu.VMEM((slots * BLOCK, 2 * HD), bf16),
            pltpu.VMEM((2, BLOCK, HD), f32),
            pltpu.VMEM((GROUP, 2, BLOCK, HD), f32),
            pltpu.VMEM((2, BLOCK, HD), f32),
            pltpu.VMEM((2, slots, BLOCK, HD), f32),
            pltpu.VMEM((2, slots, BLOCK, HD), bf16),
            pltpu.VMEM((GROUP, 2, BLOCK, HD), bf16),
            pltpu.VMEM((GROUP, 2, BLOCK, HD), bf16),
            pltpu.VMEM((CTX * slots + 1, PIECE, HD), bf16),
            pltpu.VMEM((CTX, 2, PIECE, HD), bf16),
            dma,
            dma,
            dma((2,)),
            dma((2, GROUP)),
            dma,
            dma((2,)),
            dma((2,)),
            dma,
            dma,
            dma,
            dma((2,)),
        ],
        compiler_params=pltpu.CompilerParams(
            collective_id=identity, has_side_effects=True, vmem_limit_bytes=52 << 20
        ),
        name="fused",
    )(*scalars, queries, keys, values, grads)


def on_device(queries, keys, values, grads, lengths, key_first, order):
    ids = jnp.arange(2 * CTX, dtype=jnp.int32)
    inverse = jnp.sum(jnp.where(order[None, :] == ids[:, None], ids[None, :], 0), axis=1)
    first = jnp.sum(jnp.where(order[:, None] == ids[None, :], key_first[None, :], 0), axis=1)
    counts = order - first + 1
    most = jnp.max(counts[0::2] + counts[1::2])

    def branch(slots, identity, queries, keys, values, grads):
        attended, query_grad, key_grad, value_grad = fused(
            slots, identity, (order, inverse, key_first, lengths), queries, keys, values, grads
        )
        rows = attended.shape[0]
        return attended, query_grad, key_grad.reshape(rows, HD), value_grad.reshape(rows, HD)

    return lax.cond(
        most <= 9,
        functools.partial(branch, 9, 0),
        functools.partial(branch, 2 * SPAN, 1),
        queries,
        keys,
        values,
        grads,
    )


def solution(mesh):
    return jax.shard_map(
        on_device,
        mesh=mesh,
        in_specs=(
            P(("ctx", "head"), None),
            P(("ctx", "head"), None),
            P(("ctx", "head"), None),
            P(("ctx", "head"), None),
            P(),
            P(),
            P(),
        ),
        out_specs=(P("ctx", "head"), P("ctx", "head"), P("ctx", "head"), P("ctx", "head")),
        check_vma=False,
    )
```

time: 381 us -> 85.6 us (0.22)
  waiting for transfers between devices: 192 us -> 0 us
  Pallas kernels: 0 us -> 78.8 us
  local copies, waits for them, and re-layouts: 63.7 us -> 3.81 us
  other arithmetic: 33.3 us -> 1.56 us
  matrix products: 28.7 us -> 0 us
  blocking collectives: 27.8 us -> 0 us
  between operations: 14.6 us -> 1.35 us
  loops' own time: 11.3 us -> 0.02 us
  starting transfers between devices: 7.11 us -> 0 us
    reduce_scatter x1 -> x0, waiting for transfers between devices: 120 us -> none  [on_device(): lax.psum_scatter(partials.astype(jnp.bfloat16), 'ctx', scatter_dimension=...]
    pallas_call x0 -> x1, Pallas kernels: none -> 78.8 us  [fused(): pl.pallas_call(functools.partial(fused_kernel, slots, docs), out_shape=(j...]
    all_gather x2 -> x0, waiting for transfers between devices: 54.4 us -> none  [the longest x1 53.1 us: on_device(): lax.all_gather(my_values, 'ctx', axis=0, tiled=True)]
    dot_general x28 -> x0, matrix products: 28.7 us -> none  [the longest x8 6.2 us: tile_scores(): jnp.einsum('qhgd,khd->hgqk', query_tile, key_tile, preferred_element_type...]
    all_to_all x2 -> x0, blocking collectives: 27.8 us -> none  [the longest x1 16.7 us: on_device(): lax.all_to_all(key_states, 'head', split_axis=1, concat_axis=0, tiled=True)]
    all_to_all x2 -> x0, waiting for transfers between devices: 17.4 us -> none  [the longest x1 10.4 us: on_device(): lax.all_to_all(queries, 'head', split_axis=1, concat_axis=0, tiled=True)]
    while x8 -> x0, local copies, waits for them, and re-layouts: 15.3 us -> none  [the longest x3 15.3 us: on_device(): query_sum, partials = lax.fori_loop(0, turn_count, joint_step, start_joint)]
    dynamic_update_slice x8 -> x0, other arithmetic: 13.6 us -> none  [joint_step(): lax.dynamic_update_slice_in_dim(partials, current + joined[slot_index * B...]
  transfers between devices with their start and end apart: 5 -> 0, of which waited for: 5 -> 0; matrix products, arithmetic and copies ran while one was open for 4% -> 0% of each run, Pallas kernels for 0% -> 0%
where the time goes in v2:
time: 85.6 us; the launch traced here: 85.5 us
  Pallas kernels  78.8 us (92%)
  local copies, waits for them, and re-layouts  3.81 us (4%)
  other arithmetic  1.56 us (2%)
  between operations  1.35 us (2%)
    pallas_call x1, Pallas kernels, fused(): pl.pallas_call(functools.partial(fused_kernel, slots, docs), out_shape=(j...  78.8 us
    unnamed x10, local copies, waits for them, and re-layouts  3.56 us

profile of v2, /device:TPU:1, one launch (start us, length us, event | category | flops | bytes accessed | tf_op | source)
XLA Modules:
  0.0 85.5 jit_solution(2639998679060049458)
XLA Ops:
  0.6 0.9 %select_reduce_fusion = (s32[64]{0:T(128)S(1)}, s32[64]{0:T(128)S(1)}) fusion(s32[64]{0:T(128)} %param.15, s32[64]{0:T(128)} %param.14), kind=kLoop, calls=%fused_computation | loop fusion | flops 24448 | bytes 1024 | tf_op jit(solution)/shard_map/reduce_sum | solution.py:544
  1.5 0.0 copy-start
  1.6 0.7 copy-done
  2.2 0.1 slice.7
  2.3 0.1 slice.6
  2.5 0.6 add_reduce_fusion
  3.1 0.0 copy-start.1
  3.1 0.0 copy-start.2
  3.8 0.0 copy-done.1
  3.8 0.0 copy-done.2
  3.8 78.8 %conditional.1 = ((bf16[512,512]{1,0:T(8,128)(2,1)S(1)}, bf16[512,512]{1,0:T(8,128)(2,1)S(1)}, bf16[2,256,128]{2,1,0:T(8,128)(2,1)S(1)}, bf16[2,256,128]{2,1,0:T(8,128)(2,1)S(1)})) conditional(s32[]{:T(128)} %convert_element_type.3, (s32[64]{0:T(128)S(1)}, s32[64]{0:T(128)S(1)}, s32[64]{0:T(128)S(1)}, s32[13]{0:T(128)S(1)}, ...), branch_computations={%region_3.4_spmd, %region_4.5_spmd} | conditional | bytes 8 | solution.py:556
  3.8 78.8 %fused.3 = (bf16[512,512]{1,0:T(8,128)(2,1)S(1)}, bf16[512,512]{1,0:T(8,128)(2,1)S(1)}, bf16[2,256,128]{2,1,0:T(8,128)(2,1)S(1)}, bf16[2,256,128]{2,1,0:T(8,128)(2,1)S(1)}) custom-call(s32[64]{0:T(128)S(1)} %get-tuple-element.44.order_ref, s32[64]{0:T(128)S(1)} %get-tuple-element.45.inverse_ref, s32[64]{0:T(128)S(1)} %get-tuple-element.46.first_ref, ...), custom_call_target="tpu_custom_call" | custom-call | tf_op jit(solution)/shard_map/cond/branch_1_fun/fused/pallas_call | solution.py:489
  82.6 0.8 copy.23
  83.4 0.8 copy.24
  84.2 0.7 copy.25
  84.9 0.7 copy.26
  (1 shorter events, 0.0 us)
Async XLA Ops:
  1.5 0.7 copy-start
  3.1 0.7 copy-start.1
  3.1 0.7 copy-start.2

commit v3 on v2

v3 whole, which is shorter than its diff:
```python
import functools

import jax
import jax.numpy as jnp
from jax import lax
from jax.experimental import pallas as pl
from jax.experimental.pallas import tpu as pltpu
from jax.sharding import PartitionSpec as P

HD = 128
BLOCK = 256
SPAN = 7
CTX = 32
HEADS = 8
GROUP = 4
ROWS = 64
PIECE = 16
MESH = pl.DeviceIdType.MESH
LOG2E = 1.4426950408889634
SCALE = HD**-0.5
AHEAD = 4
EARLY = 2
LAST = (((1,), (1,)), ((), ()))
FIRST = (((0,), (0,)), ((), ()))


def drain(ref, sem):
    pltpu.make_async_copy(ref, ref, sem).wait()


def loop(count, body):
    def step(index, carry):
        body(index)
        return carry

    lax.fori_loop(0, count, step, 0)


def greet(me, head):
    barrier = pltpu.get_barrier_semaphore()
    chip = lax.div(me, 2)

    def signal(ctx, z):
        pl.semaphore_signal(barrier, inc=1, device_id=(ctx, z), device_id_type=MESH)

    loop(CTX - 1, lambda r: signal(lax.rem(me + r + 1, CTX), head))
    loop(HEADS - 1, lambda r: signal(me, lax.rem(head + r + 1, HEADS)))
    for half in range(2):
        source = half * 4 + lax.div(chip, 4)
        loop(CTX - 1, lambda r: signal(lax.rem(me + r + 1, CTX), source))

        @pl.when(source != head)
        def _():
            signal(me, source)

    apart = lax.rem(lax.div(chip, 4) + 4 - lax.rem(head, 4), 4)
    pl.semaphore_wait(barrier, CTX - 1 + HEADS - 1 + 2 * CTX - 1 + lax.div(apart + 3, 4))


def fused_kernel(
    slots,
    docs,
    order_ref,
    inverse_ref,
    first_ref,
    lengths_ref,
    q_ref,
    k_ref,
    v_ref,
    g_ref,
    o_ref,
    dq_ref,
    dk_ref,
    dv_ref,
    table,
    q_buf,
    g_buf,
    g_scaled,
    turned,
    o_turned,
    kv,
    pieces,
    staged,
    bias,
    scores,
    probs,
    grads,
    wide_keys,
    wide_values,
    maxima,
    totals,
    inverses,
    inverse_rows,
    delta,
    sums,
    part,
    o_buf,
    dq_buf,
    arrived,
    summed,
    landed,
    piece_send,
    piece_recv,
    wide_send,
    wide_recv,
    list_send,
    list_recv,
    out_sem,
    part_send,
    part_recv,
    sum_send,
    sum_recv,
):
    me = lax.axis_index("ctx")
    head = lax.axis_index("head")
    chip, kind = lax.div(me, 2), lax.rem(me, 2)
    greet(me, head)

    def remote(src, dst, send, recv, ctx, z):
        pltpu.make_async_remote_copy(
            src_ref=src,
            dst_ref=dst,
            send_sem=send,
            recv_sem=recv,
            device_id=(ctx, z),
            device_id_type=MESH,
        ).start()

    pair = lax.div(head, 4)

    def send_pieces(which):
        ref = (k_ref, v_ref)[which]
        slot = pieces.at[me * 2 + pair]

        def piece(p, z):
            rows = pl.ds(pl.multiple_of(p * PIECE, PIECE), PIECE)
            return ref.at[rows, pl.ds(pl.multiple_of(z * HD, HD), HD)]

        def target(p):
            return (lax.rem(head, 4) * 4 + p) * 2 + which

        def send_piece(r):
            p, z = lax.rem(r, 4), lax.rem(head + lax.div(r, 4) + 1, HEADS)
            remote(piece(p, z), slot, piece_send, piece_recv, target(p), z)

        loop(4 * (HEADS - 1), send_piece)
        for p in range(4):

            @pl.when(target(p) != me)
            def _(p=p):
                remote(piece(p, head), slot, piece_send, piece_recv, target(p), head)

            @pl.when(target(p) == me)
            def _(p=p):
                pltpu.make_async_copy(piece(p, head), slot, piece_recv).start()

    send_pieces(0)
    send_pieces(1)

    my_rows = pl.ds(pl.multiple_of(lax.rem(head, 4) * ROWS, ROWS), ROWS)

    def columns(z, g):
        return pl.ds(pl.multiple_of(z * GROUP * HD + g * HD, HD), HD)

    def send_chunk(chunk):
        which, g = divmod(chunk, GROUP)
        ref, buf = ((q_ref, q_buf), (g_ref, g_buf))[which]

        def send_wide(r):
            z = lax.rem(head + r + 1, HEADS)
            remote(
                ref.at[:, columns(z, g)],
                buf.at[g, pair, my_rows],
                wide_send.at[which],
                wide_recv.at[which, g],
                me,
                z,
            )

        loop(HEADS - 1, send_wide)
        pltpu.make_async_copy(
            ref.at[:, columns(head, g)], buf.at[g, pair, my_rows], wide_recv.at[which, g]
        ).start()

    def take_chunk(chunk):
        which, g = divmod(chunk, GROUP)
        drain((q_buf, g_buf)[which].at[g], wide_recv.at[which, g])
        if chunk + AHEAD < 2 * GROUP:
            send_chunk(chunk + AHEAD)

    for chunk in range(AHEAD):
        send_chunk(chunk)

    rows = lax.broadcasted_iota(jnp.int32, (BLOCK, BLOCK), 0)
    cols = lax.broadcasted_iota(jnp.int32, (BLOCK, BLOCK), 1)

    def pair_of(device):
        block_a, block_b = order_ref[2 * device], order_ref[2 * device + 1]
        return block_a, block_b, block_a - first_ref[block_a] + 1

    block_a, block_b, count_a = pair_of(me)
    count_b = block_b - first_ref[block_b] + 1

    def belongs(t):
        return (t == 1) | (t > count_a)

    def chosen(t):
        return belongs(t).astype(jnp.int32)

    def make_bias(t):
        late = belongs(t)
        block = jnp.where(late, block_b, block_a)
        back = jnp.where(t < 2, 0, jnp.where(late, t - count_a, t - 1))
        reach = jnp.where(t < count_a + count_b, back * BLOCK, -2 * BLOCK)
        low = jnp.zeros((BLOCK, BLOCK), jnp.int32)
        end = 0
        for doc in range(docs - 1):
            end = end + lengths_ref[doc]
            low = jnp.where(cols + block * BLOCK >= end, end, low)
        allowed = (rows + (block - back) * BLOCK >= low) & (rows - cols <= reach)
        bias[t] = jnp.where(allowed, 0.0, -jnp.inf)

    def rows_of(device):
        return pl.ds(pl.multiple_of(lax.div(device, 2) * PIECE, PIECE), PIECE)

    def send_lists():
        def stage(peer):
            first_block, second_block, first_count = pair_of(peer)
            for slot in range(slots):
                if slot < 2:
                    wanted = (first_block, second_block)[slot]
                else:
                    wanted = jnp.where(
                        slot <= first_count,
                        first_block - slot + 1,
                        second_block - slot + first_count,
                    )
                staged[peer, slot] = pieces[inverse_ref[jnp.maximum(wanted, 0)]]

        def send_list(r):
            peer = lax.rem(me + r + 1, CTX)
            stage(peer)
            remote(
                staged.at[peer],
                kv.at[kind, :, rows_of(me)],
                list_send,
                list_recv.at[kind],
                peer,
                head,
            )

        loop(CTX - 1, send_list)
        stage(me)
        pltpu.make_async_copy(
            staged.at[me], kv.at[kind, :, rows_of(me)], list_recv.at[kind]
        ).start()

    def first_round():
        drain(pieces, piece_recv)
        send_lists()

    pl.when(kind == 0)(first_round)
    take_chunk(0)
    loop(slots, make_bias)
    take_chunk(1)
    drain(kv.at[0], list_recv.at[0])

    def second_round():
        drain(pieces, piece_recv)
        send_lists()

    pl.when(kind == 1)(second_round)

    zeros = jnp.zeros((HD, BLOCK), jnp.bfloat16)

    def widen(wide, which, t):
        turned = kv[which, t].T
        for i, flag in enumerate((~belongs(t), belongs(t))):
            wide[i * HD : (i + 1) * HD, tile_cols(t)] = jnp.where(flag, turned, zeros)

    unroll = 3 if slots % 3 == 0 else 2

    def tiles(body):
        def several(index):
            for u in range(unroll):
                body(index * unroll + u)

        loop(slots // unroll, several)

    def tile_cols(t):
        return pl.ds(pl.multiple_of(t * BLOCK, BLOCK), BLOCK)

    def fold(tile, combine):
        height = tile.shape[0]
        while height > 8:
            height //= 2
            tile = combine(tile[:height], tile[height:])
        return tile

    def send_out(buf, ref, g, which):
        for i in range(2):
            pltpu.make_async_copy(
                buf.at[g, i],
                ref.at[pl.ds(i * BLOCK, BLOCK), pl.ds(pl.multiple_of(g * HD, HD), HD)],
                out_sem.at[which],
            ).start()

    def forward(g):
        for i in range(2):
            turned[i] = q_buf[g, i].T
        maxima[...] = jnp.full_like(maxima, -jnp.inf)
        totals[...] = jnp.zeros_like(totals)

        def score(t):
            tile = jnp.dot(kv[0, t], turned[chosen(t)], preferred_element_type=jnp.float32)
            tile = tile + bias[t]
            scores[t] = tile
            top = fold(tile, jnp.maximum)
            for i in range(2):
                penalty = jnp.where(chosen(t) == i, 0.0, -jnp.inf)
                maxima[i] = jnp.maximum(maxima[i], top + penalty)

        tiles(score)
        for i in range(2):
            top = jnp.max(maxima[i], axis=0, keepdims=True) * (SCALE * LOG2E)
            maxima[i] = jnp.broadcast_to(top, (8, BLOCK))

        def weigh(t):
            tile = jnp.exp2(scores[t] * (SCALE * LOG2E) - maxima[chosen(t), :1])
            probs[g, tile_cols(t)] = tile.astype(jnp.bfloat16)
            part_sum = fold(tile, jnp.add)
            late = belongs(t).astype(jnp.float32)
            for i, flag in enumerate((1.0 - late, late)):
                totals[i] = totals[i] + part_sum * flag

        tiles(weigh)
        for i in range(2):
            inverse = 1.0 / jnp.sum(totals[i], axis=0, keepdims=True)
            inverses[g, i] = jnp.broadcast_to(inverse, (8, BLOCK))
            inverse_rows[g, i] = jnp.broadcast_to(inverse, (HD, BLOCK)).T

    def attend(g):
        both = jnp.dot(wide_values[...], probs[g], preferred_element_type=jnp.float32)
        for i in range(2):
            result = both[i * HD : (i + 1) * HD] * inverses[g, i, :1]
            o_turned[g, i] = result.astype(jnp.bfloat16)
            o_buf[g, i] = result.T.astype(jnp.bfloat16)
        send_out(o_buf, o_ref, g, 0)

    def prepare(g):
        for i in range(2):
            scaled = (g_buf[g, i].astype(jnp.float32) * inverse_rows[g, i]).astype(jnp.bfloat16)
            g_scaled[g, i] = scaled

    def turn(g):
        for i in range(2):
            turned[i] = g_scaled[g, i].T
            product = o_turned[g, i].astype(jnp.float32) * turned[i].astype(jnp.float32)
            total = jnp.sum(fold(product, jnp.add), axis=0, keepdims=True)
            delta[i] = jnp.broadcast_to(total, (8, BLOCK))

    def value_grad(g, store):
        def step(t):
            store(
                t,
                jnp.dot(
                    probs[g, tile_cols(t)],
                    g_scaled[g, chosen(t)],
                    preferred_element_type=jnp.float32,
                ),
            )

        tiles(step)

    def key_grad(g, store):
        def step(t):
            prob_grad = jnp.dot(kv[1, t], turned[chosen(t)], preferred_element_type=jnp.float32)
            score_grad = (
                probs[g, tile_cols(t)].astype(jnp.float32)
                * (prob_grad - delta[chosen(t), :1])
            ).astype(jnp.bfloat16)
            grads[g, tile_cols(t)] = score_grad
            store(
                t, jnp.dot(score_grad, q_buf[g, chosen(t)], preferred_element_type=jnp.float32)
            )

        tiles(step)

    def query_grad(g):
        both = jnp.dot(wide_keys[...], grads[g], preferred_element_type=jnp.float32)
        for i in range(2):
            dq_buf[g, i] = (both[i * HD : (i + 1) * HD] * SCALE).T.astype(jnp.bfloat16)
        send_out(dq_buf, dq_ref, g, 1)

    sums[...] = jnp.zeros_like(sums)
    others = slots - 2

    def keep(which):
        def store(t, value):
            sums[which, t] = sums[which, t] + value

        return store

    def finish(which, factor):
        def store(t, value):
            part[which, t] = ((sums[which, t] + value) * factor).astype(jnp.bfloat16)

        return store

    def send_parts(which):
        def send_part(peer_chip, core):
            peer = peer_chip * 2 + core
            remote(
                part.at[which, pl.ds(2, others), rows_of(peer)],
                arrived.at[pl.ds(me * others, others)],
                part_send,
                part_recv,
                peer,
                head,
            )

        loop(15, lambda r: send_part(lax.rem(chip + r + 1, 16), which))

        @pl.when(kind != which)
        def _():
            send_part(chip, which)

        @pl.when(kind == which)
        def _():
            pltpu.make_async_copy(
                part.at[which, pl.ds(2, others), rows_of(me)],
                arrived.at[pl.ds(me * others, others)],
                part_recv,
            ).start()

    loop(slots, functools.partial(widen, wide_keys, 0))
    for g in range(GROUP):
        if g >= 2:
            take_chunk(g)
        forward(g)
    for g in range(GROUP - 1):
        take_chunk(GROUP + g)
        prepare(g)
        value_grad(g, keep(1))
    drain(kv.at[1], list_recv.at[1])
    loop(slots, functools.partial(widen, wide_values, 1))
    loop(GROUP, attend)

    def early(g):
        turn(g)
        key_grad(g, keep(0))

    loop(EARLY, early)
    take_chunk(2 * GROUP - 1)
    prepare(GROUP - 1)
    value_grad(GROUP - 1, finish(1, 1.0))
    send_parts(1)
    loop(GROUP - 1 - EARLY, lambda g: early(g + EARLY))
    turn(GROUP - 1)
    key_grad(GROUP - 1, finish(0, SCALE))
    send_parts(0)
    loop(GROUP, query_grad)

    nowhere = CTX * others

    def make_table(place):
        block = order_ref[place]
        for step in range(SPAN - 1):
            query = jnp.minimum(block + step + 1, 2 * CTX - 1)
            spot = inverse_ref[query]
            device = lax.div(spot, 2)
            ahead = jnp.where(lax.rem(spot, 2) == 1, pair_of(device)[2] - 1, 0)
            listed = (block + step + 1 == query) & (first_ref[query] <= block)
            table[place * SPAN + step] = jnp.where(listed, device * others + ahead + step, nowhere)

    loop(2 * CTX, make_table)
    arrived[nowhere] = jnp.zeros(arrived.shape[1:], arrived.dtype)
    drain(arrived.at[pl.ds(0, nowhere)], part_recv)

    def add_up(peer):
        for block in range(2):
            first = (peer * 2 + block) * SPAN
            total = arrived[table[first]].astype(jnp.float32)
            for step in range(1, SPAN - 1):
                total = total + arrived[table[first + step]].astype(jnp.float32)
            summed[peer, block] = total.astype(summed.dtype)

    def send_sum(r):
        peer = lax.rem(me + r + 1, CTX)
        add_up(peer)
        remote(
            summed.at[peer],
            landed.at[kind, :, rows_of(me)],
            sum_send,
            sum_recv.at[kind],
            peer,
            head,
        )

    loop(CTX - 1, send_sum)
    add_up(me)
    pltpu.make_async_copy(
        summed.at[me], landed.at[kind, :, rows_of(me)], sum_recv.at[kind]
    ).start()

    drain(pieces.at[pl.ds(0, ROWS - 1)], piece_send)

    @pl.when(lax.div(chip, 4) != lax.rem(head, 4))
    def _():
        drain(pieces.at[0], piece_send)

    for buf, which in ((q_buf, 0), (g_buf, 1)):
        for g in range(GROUP):
            drain(buf.at[g, 0], wide_send.at[which])
            drain(buf.at[g, 1, pl.ds(0, 3 * ROWS)], wide_send.at[which])
    drain(staged.at[pl.ds(0, CTX - 1)], list_send)
    drain(arrived.at[pl.ds(0, (CTX - 1) * others)], part_send)
    drain(summed.at[pl.ds(0, CTX - 1)], sum_send)
    drain(o_buf, out_sem.at[0])
    drain(dq_buf, out_sem.at[1])
    for which, out_ref in ((1, dv_ref), (0, dk_ref)):
        drain(landed.at[which], sum_recv.at[which])
        for i in range(2):
            total = landed[which, i].astype(jnp.float32) + part[which, i].astype(jnp.float32)
            out_ref[i] = total.astype(jnp.bfloat16)


def fused(slots, identity, scalars, queries, keys, values, grads):
    docs = scalars[-1].shape[0]
    anywhere = pl.BlockSpec(memory_space=pl.ANY)
    small = pl.BlockSpec(memory_space=pltpu.SMEM)
    bf16, f32 = jnp.bfloat16, jnp.float32
    rows, wide = ROWS * HEADS, GROUP * HD
    dma = pltpu.SemaphoreType.DMA
    return pl.pallas_call(
        functools.partial(fused_kernel, slots, docs),
        out_shape=(
            jax.ShapeDtypeStruct((rows, wide), bf16),
            jax.ShapeDtypeStruct((rows, wide), bf16),
            jax.ShapeDtypeStruct((2, BLOCK, HD), bf16),
            jax.ShapeDtypeStruct((2, BLOCK, HD), bf16),
        ),
        in_specs=[small] * 4 + [anywhere] * 4,
        out_specs=[anywhere] * 2 + [pl.BlockSpec(memory_space=pltpu.VMEM)] * 2,
        scratch_shapes=[
            pltpu.SMEM((2 * CTX * SPAN,), jnp.int32),
            pltpu.VMEM((GROUP, 2, BLOCK, HD), bf16),
            pltpu.VMEM((GROUP, 2, BLOCK, HD), bf16),
            pltpu.VMEM((GROUP, 2, BLOCK, HD), bf16),
            pltpu.VMEM((2, HD, BLOCK), bf16),
            pltpu.VMEM((GROUP, 2, HD, BLOCK), bf16),
            pltpu.VMEM((2, slots, BLOCK, HD), bf16),
            pltpu.VMEM((2 * CTX, PIECE, HD), bf16),
            pltpu.VMEM((CTX, slots, PIECE, HD), bf16),
            pltpu.VMEM((slots, BLOCK, BLOCK), f32),
            pltpu.VMEM((slots, BLOCK, BLOCK), f32),
            pltpu.VMEM((GROUP, slots * BLOCK, BLOCK), bf16),
            pltpu.VMEM((GROUP, slots * BLOCK, BLOCK), bf16),
            pltpu.VMEM((2 * HD, slots * BLOCK), bf16),
            pltpu.VMEM((2 * HD, slots * BLOCK), bf16),
            pltpu.VMEM((2, 8, BLOCK), f32),
            pltpu.VMEM((2, 8, BLOCK), f32),
            pltpu.VMEM((GROUP, 2, 8, BLOCK), f32),
            pltpu.VMEM((GROUP, 2, BLOCK, HD), f32),
            pltpu.VMEM((2, 8, BLOCK), f32),
            pltpu.VMEM((2, slots, BLOCK, HD), f32),
            pltpu.VMEM((2, slots, BLOCK, HD), bf16),
            pltpu.VMEM((GROUP, 2, BLOCK, HD), bf16),
            pltpu.VMEM((GROUP, 2, BLOCK, HD), bf16),
            pltpu.VMEM((CTX * (slots - 2) + 1, PIECE, HD), bf16),
            pltpu.VMEM((CTX, 2, PIECE, HD), bf16),
            pltpu.VMEM((2, 2, BLOCK, HD), bf16),
            dma,
            dma,
            dma((2,)),
            dma((2, GROUP)),
            dma,
            dma((2,)),
            dma((2,)),
            dma,
            dma,
            dma,
            dma((2,)),
        ],
        compiler_params=pltpu.CompilerParams(
            collective_id=identity, has_side_effects=True, vmem_limit_bytes=52 << 20
        ),
        name="fused",
    )(*scalars, queries, keys, values, grads)


def deliver_kernel(*refs):
    half = len(refs) // 2
    copies = [
        pltpu.make_async_copy(refs[i], refs[half + i], refs[2 * half].at[i]) for i in range(half)
    ]
    for copy in copies:
        copy.start()
    for copy in copies:
        copy.wait()


def deliver(*results):
    anywhere = pl.BlockSpec(memory_space=pl.ANY)
    return pl.pallas_call(
        deliver_kernel,
        out_shape=tuple(jax.ShapeDtypeStruct(r.shape, r.dtype) for r in results),
        in_specs=[anywhere] * len(results),
        out_specs=[anywhere] * len(results),
        scratch_shapes=[pltpu.SemaphoreType.DMA((len(results),))],
        name="deliver",
    )(*results)


def on_device(queries, keys, values, grads, lengths, key_first, order):
    ids = jnp.arange(2 * CTX, dtype=jnp.int32)
    inverse = jnp.sum(jnp.where(order[None, :] == ids[:, None], ids[None, :], 0), axis=1)
    first = jnp.sum(jnp.where(order[:, None] == ids[None, :], key_first[None, :], 0), axis=1)
    counts = order - first + 1
    most = jnp.max(counts[0::2] + counts[1::2])

    def branch(slots, identity, queries, keys, values, grads):
        attended, query_grad, key_grad, value_grad = fused(
            slots, identity, (order, inverse, key_first, lengths), queries, keys, values, grads
        )
        rows = attended.shape[0]
        return attended, query_grad, key_grad.reshape(rows, HD), value_grad.reshape(rows, HD)

    results = lax.cond(
        most <= 9,
        functools.partial(branch, 9, 0),
        functools.partial(branch, 2 * SPAN, 1),
        queries,
        keys,
        values,
        grads,
    )
    return deliver(*results)


def solution(mesh):
    return jax.shard_map(
        on_device,
        mesh=mesh,
        in_specs=(
            P(("ctx", "head"), None),
            P(("ctx", "head"), None),
            P(("ctx", "head"), None),
            P(("ctx", "head"), None),
            P(),
            P(),
            P(),
        ),
        out_specs=(P("ctx", "head"), P("ctx", "head"), P("ctx", "head"), P("ctx", "head")),
        check_vma=False,
    )
```

time: 85.6 us -> 75.7 us (0.88)
  Pallas kernels: 78.8 us -> 71.7 us
  local copies, waits for them, and re-layouts: 3.81 us -> 0.91 us
    pallas_call x1, Pallas kernels: 78.8 us -> 70.6 us  [fused(): pl.pallas_call(functools.partial(fused_kernel, slots, docs), out_shape=(j...]
    unnamed x10 -> x6, local copies, waits for them, and re-layouts: 3.56 us -> 0.65 us
    pallas_call x0 -> x1, Pallas kernels: none -> 1.08 us  [deliver(): pl.pallas_call(deliver_kernel, out_shape=tuple((jax.ShapeDtypeStruct(r.sh...]
    reduce_sum x0 -> x1, other arithmetic: none -> 0.89 us  [on_device(): jnp.sum(jnp.where(order[:, None] == ids[None, :], key_first[None, :], 0),...]
where the time goes in v3:
time: 75.7 us; the launch traced here: 75.6 us
  Pallas kernels  71.7 us (95%)
  other arithmetic  1.65 us (2%)
  between operations  1.36 us (2%)
  local copies, waits for them, and re-layouts  0.91 us (1%)
    pallas_call x1, Pallas kernels, fused(): pl.pallas_call(functools.partial(fused_kernel, slots, docs), out_shape=(j...  70.6 us

profile of v3, /device:TPU:1, one launch (start us, length us, event | category | flops | bytes accessed | tf_op | source)
XLA Modules:
  0.0 75.6 jit_solution(6303775451300594501)
XLA Ops:
  0.6 0.0 copy-start
  0.6 0.9 %select_reduce_fusion.2 = s32[64]{0:T(128)S(1)} fusion(s32[64]{0:T(128)} %param.14, s32[64]{0:T(128)} %param.15), kind=kLoop, calls=%fused_computation.2 | loop fusion | flops 12224 | bytes 768 | tf_op jit(solution)/shard_map/reduce_sum | solution.py:618
  1.5 0.0 copy-done
  1.6 0.1 slice.7
  1.7 0.1 slice.6
  1.8 0.6 add_reduce_fusion
  3.1 0.0 copy-start.1
  3.1 0.0 copy-start.2
  3.2 0.6 copy-done.1
  3.8 0.0 copy-done.2
  3.8 70.7 %conditional.1 = ((bf16[512,512]{1,0:T(8,128)(2,1)S(1)}, bf16[512,512]{1,0:T(8,128)(2,1)S(1)}, bf16[2,256,128]{2,1,0:T(8,128)(2,1)S(1)}, bf16[2,256,128]{2,1,0:T(8,128)(2,1)S(1)})) conditional(s32[]{:T(128)} %convert_element_type.3, (s32[64]{0:T(128)S(1)}, s32[64]{0:T(128)S(1)}, s32[64]{0:T(128)S(1)}, s32[13]{0:T(128)S(1)}, ...), branch_computations={%region_3.4_spmd, %region_4.5_spmd} | conditional | flops 12224 | bytes 49676 | solution.py:629
  3.8 0.1 select_reduce_fusion.1.inverse_ref
  3.9 70.6 %fused.3 = (bf16[512,512]{1,0:T(8,128)(2,1)S(1)}, bf16[512,512]{1,0:T(8,128)(2,1)S(1)}, bf16[2,256,128]{2,1,0:T(8,128)(2,1)S(1)}, bf16[2,256,128]{2,1,0:T(8,128)(2,1)S(1)}) custom-call(s32[64]{0:T(128)S(1)} %get-tuple-element.106, s32[64]{0:T(128)S(1)} %select_reduce_fusion.1.inverse_ref, s32[64]{0:T(128)S(1)} %get-tuple-element.43.first_ref, ...), custom_call_target="tpu_custom_call" | custom-call | tf_op jit(solution)/shard_map/cond/branch_1_fun/fused/pallas_call | solution.py:535
  74.5 1.1 %deliver.1 = (bf16[512,512]{1,0:T(8,128)(2,1)}, bf16[512,512]{1,0:T(8,128)(2,1)}, bf16[512,128]{1,0:T(8,128)(2,1)}, bf16[512,128]{1,0:T(8,128)(2,1)}) custom-call(bf16[512,512]{1,0:T(8,128)(2,1)S(1)} %get-tuple-element.111.refs_0_, bf16[512,512]{1,0:T(8,128)(2,1)S(1)} %get-tuple-element.110.refs_1_, bf16[512,128]{1,0:T(8,128)(2,1)S(1)} %bitcast.2, ...), custom_call_target="tpu_custom_call" | custom-call | tf_op jit(solution)/shard_map/deliver/pallas_call | solution.py:605
  (4 shorter events, 0.0 us)
Async XLA Ops:
  0.6 0.9 %copy-start = (s32[64]{0:T(128)S(1)}, s32[64]{0:T(128)}, u32[]{:S(2)}) copy-start(s32[64]{0:T(128)} %param.15) | copy-start | bytes 772
  3.1 0.7 copy-start.1
  3.1 0.7 copy-start.2

commit v4 on v3

--- a/solution.py
+++ b/solution.py
@@ -10,6 +10,7 @@
 HD = 128
 BLOCK = 256
 SPAN = 7
+SHORT = 9
 CTX = 32
 HEADS = 8
 GROUP = 4
@@ -18,7 +19,7 @@
 MESH = pl.DeviceIdType.MESH
 LOG2E = 1.4426950408889634
 SCALE = HD**-0.5
-AHEAD = 4
+AHEAD = 6
 EARLY = 2
 LAST = (((1,), (1,)), ((), ()))
 FIRST = (((0,), (0,)), ((), ()))
@@ -34,6 +35,17 @@
         return carry
 
     lax.fori_loop(0, count, step, 0)
+
+
+def grouped(count, ready, send):
+    def several(first, size):
+        for u in range(size):
+            ready(first + u)
+        for u in range(size):
+            send(first + u)
+
+    loop(count // 4, lambda index: several(index * 4, 4))
+    several(count // 4 * 4, count % 4)
 
 
 def greet(me, head):
@@ -72,6 +84,7 @@
     dq_ref,
     dk_ref,
     dv_ref,
+    most_ref,
     table,
     q_buf,
     g_buf,
@@ -239,7 +252,6 @@
 
         def send_list(r):
             peer = lax.rem(me + r + 1, CTX)
-            stage(peer)
             remote(
                 staged.at[peer],
                 kv.at[kind, :, rows_of(me)],
@@ -249,7 +261,7 @@
                 head,
             )
 
-        loop(CTX - 1, send_list)
+        grouped(CTX - 1, lambda r: stage(lax.rem(me + r + 1, CTX)), send_list)
         stage(me)
         pltpu.make_async_copy(
             staged.at[me], kv.at[kind, :, rows_of(me)], list_recv.at[kind]
@@ -263,6 +275,12 @@
     take_chunk(0)
     loop(slots, make_bias)
     take_chunk(1)
+
+    def tile_count(device, most):
+        first_block, second_block, first_count = pair_of(device)
+        return jnp.maximum(most, first_count + second_block - first_ref[second_block] + 1)
+
+    most_ref[0] = lax.fori_loop(0, CTX, tile_count, 0)
     drain(kv.at[0], list_recv.at[0])
 
     def second_round():
@@ -471,7 +489,8 @@
             device = lax.div(spot, 2)
             ahead = jnp.where(lax.rem(spot, 2) == 1, pair_of(device)[2] - 1, 0)
             listed = (block + step + 1 == query) & (first_ref[query] <= block)
-            table[place * SPAN + step] = jnp.where(listed, device * others + ahead + step, nowhere)
+            spot = jnp.minimum(device * others + ahead + step, nowhere)
+            table[place * SPAN + step] = jnp.where(listed, spot, nowhere)
 
     loop(2 * CTX, make_table)
     arrived[nowhere] = jnp.zeros(arrived.shape[1:], arrived.dtype)
@@ -487,7 +506,6 @@
 
     def send_sum(r):
         peer = lax.rem(me + r + 1, CTX)
-        add_up(peer)
         remote(
             summed.at[peer],
             landed.at[kind, :, rows_of(me)],
@@ -497,7 +515,7 @@
             head,
         )
 
-    loop(CTX - 1, send_sum)
+    grouped(CTX - 1, lambda r: add_up(lax.rem(me + r + 1, CTX)), send_sum)
     add_up(me)
     pltpu.make_async_copy(
         summed.at[me], landed.at[kind, :, rows_of(me)], sum_recv.at[kind]
@@ -539,9 +557,10 @@
             jax.ShapeDtypeStruct((rows, wide), bf16),
             jax.ShapeDtypeStruct((2, BLOCK, HD), bf16),
             jax.ShapeDtypeStruct((2, BLOCK, HD), bf16),
+            jax.ShapeDtypeStruct((1,), jnp.int32),
         ),
         in_specs=[small] * 4 + [anywhere] * 4,
-        out_specs=[anywhere] * 2 + [pl.BlockSpec(memory_space=pltpu.VMEM)] * 2,
+        out_specs=[anywhere] * 2 + [pl.BlockSpec(memory_space=pltpu.VMEM)] * 2 + [small],
         scratch_shapes=[
             pltpu.SMEM((2 * CTX * SPAN,), jnp.int32),
             pltpu.VMEM((GROUP, 2, BLOCK, HD), bf16),
@@ -615,27 +634,22 @@
 def on_device(queries, keys, values, grads, lengths, key_first, order):
     ids = jnp.arange(2 * CTX, dtype=jnp.int32)
     inverse = jnp.sum(jnp.where(order[None, :] == ids[:, None], ids[None, :], 0), axis=1)
-    first = jnp.sum(jnp.where(order[:, None] == ids[None, :], key_first[None, :], 0), axis=1)
-    counts = order - first + 1
-    most = jnp.max(counts[0::2] + counts[1::2])
-
-    def branch(slots, identity, queries, keys, values, grads):
-        attended, query_grad, key_grad, value_grad = fused(
-            slots, identity, (order, inverse, key_first, lengths), queries, keys, values, grads
-        )
-        rows = attended.shape[0]
-        return attended, query_grad, key_grad.reshape(rows, HD), value_grad.reshape(rows, HD)
-
-    results = lax.cond(
-        most <= 9,
-        functools.partial(branch, 9, 0),
-        functools.partial(branch, 2 * SPAN, 1),
-        queries,
-        keys,
-        values,
-        grads,
+    scalars = (order, inverse, key_first, lengths)
+    *results, most = fused(SHORT, 0, scalars, queries, keys, values, grads)
+
+    def deliver_results(*results):
+        rows = results[0].shape[0]
+        return deliver(*(r.reshape(rows, r.shape[-1]) for r in results))
+
+    def enough(results, arrays):
+        return deliver_results(*results)
+
+    def general(results, arrays):
+        return deliver_results(*fused(2 * SPAN, 1, scalars, *arrays)[:4])
+
+    return lax.cond(
+        most[0] <= SHORT, enough, general, results, (queries, keys, values, grads)
     )
-    return deliver(*results)
 
 
 def solution(mesh):

time: 75.7 us -> 73.3 us (0.968)
  Pallas kernels: 71.7 us -> 70.5 us
  other arithmetic: 1.65 us -> 0.76 us
    pallas_call x1, Pallas kernels: 70.6 us -> 69.4 us  [fused(): pl.pallas_call(functools.partial(fused_kernel, slots, docs), out_shape=(j...]
    reduce_sum x1 -> x0, other arithmetic: 0.89 us -> none  [on_device(): jnp.sum(jnp.where(order[:, None] == ids[None, :], key_first[None, :], 0),...]
where the time goes in v4:
time: 73.3 us; the launch traced here: 73.2 us
  Pallas kernels  70.5 us (96%)
  between operations  1.27 us (2%)
  other arithmetic  0.76 us (1%)
    pallas_call x1, Pallas kernels, fused(): pl.pallas_call(functools.partial(fused_kernel, slots, docs), out_shape=(j...  69.4 us

profile of v4, /device:TPU:1, one launch (start us, length us, event | category | flops | bytes accessed | tf_op | source)
XLA Modules:
  0.0 73.2 jit_solution(577658019935355106)
XLA Ops:
  0.6 0.8 %select_reduce_fusion.inverse_ref = s32[64]{0:T(128)S(1)} fusion(s32[64]{0:T(128)} %order_ref.1), kind=kLoop, calls=%fused_computation | loop fusion | flops 12224 | bytes 512 | tf_op jit(solution)/shard_map/reduce_sum | solution.py:636
  1.4 0.0 copy-start.8
  1.4 0.0 copy-start.9
  1.4 0.0 copy-start.10
  1.4 0.6 copy-done.8
  2.1 0.0 copy-done.9
  2.1 0.0 copy-done.10
  2.1 0.0 copy-start.4
  2.1 0.0 copy-start.5
  2.1 0.0 copy-start.6
  2.1 0.0 copy-start.7
  2.1 69.4 %fused.3 = (bf16[512,512]{1,0:T(8,128)(2,1)S(1)}, bf16[512,512]{1,0:T(8,128)(2,1)S(1)}, bf16[2,256,128]{2,1,0:T(8,128)(2,1)S(1)}, bf16[2,256,128]{2,1,0:T(8,128)(2,1)S(1)}, s32[1]{0:T(128)}) custom-call(s32[64]{0:T(128)S(1)} %copy-done.8, s32[64]{0:T(128)S(1)} %select_reduce_fusion.inverse_ref, s32[64]{0:T(128)S(1)} %copy-done.9, s32[13]{0:T(128)S(1)} %copy-done.10, ...), custom_call_target="tpu_custom_call" | custom-call | tf_op jit(solution)/shard_map/fused/pallas_call | solution.py:553
  72.1 0.0 copy-done.4
  72.1 0.0 copy-done.5
  72.1 0.0 copy-done.6
  72.1 0.0 copy-done.7
  72.1 1.1 %conditional.1 = ((bf16[512,512]{1,0:T(8,128)(2,1)}, bf16[512,512]{1,0:T(8,128)(2,1)}, bf16[512,128]{1,0:T(8,128)(2,1)}, bf16[512,128]{1,0:T(8,128)(2,1)})) conditional(s32[]{:T(128)} %bitcast.4, (s32[64]{0:T(128)S(1)}, s32[64]{0:T(128)S(1)}, s32[64]{0:T(128)S(1)}, s32[13]{0:T(128)S(1)}, bf16[64,4096]{1,0:T(8,128)(2,1)S(1)}, ...), branch_computations={%region_1.2_spmd, %region_2.3_spmd} | conditional | bytes 5243000 | solution.py:650
  72.1 1.1 %deliver.3 = (bf16[512,512]{1,0:T(8,128)(2,1)}, bf16[512,512]{1,0:T(8,128)(2,1)}, bf16[512,128]{1,0:T(8,128)(2,1)}, bf16[512,128]{1,0:T(8,128)(2,1)}) custom-call(bf16[512,512]{1,0:T(8,128)(2,1)S(1)} %get-tuple-element.36.refs_0_, bf16[512,512]{1,0:T(8,128)(2,1)S(1)} %get-tuple-element.37.refs_1_, bf16[512,128]{1,0:T(8,128)(2,1)S(1)} %bitcast.7, ...), custom_call_target="tpu_custom_call" | custom-call | tf_op jit(solution)/shard_map/cond/branch_1_fun/deliver/pallas_call | solution.py:624
Async XLA Ops:
  1.4 0.7 copy-start.8
  1.4 0.7 copy-start.9
  1.4 0.7 copy-start.10
  2.1 70.0 %copy-start.4 = (bf16[64,4096]{1,0:T(8,128)(2,1)S(1)}, bf16[64,4096]{1,0:T(8,128)(2,1)}, u32[]{:S(2)}) copy-start(bf16[64,4096]{1,0:T(8,128)(2,1)} %q_ref.1) | copy-start | bytes 1572868
  2.1 70.0 %copy-start.5 = (bf16[64,4096]{1,0:T(8,128)(2,1)S(1)}, bf16[64,4096]{1,0:T(8,128)(2,1)}, u32[]{:S(2)}) copy-start(bf16[64,4096]{1,0:T(8,128)(2,1)} %g_ref.1) | copy-start | bytes 1572868
  2.1 70.0 %copy-start.6 = (bf16[64,1024]{1,0:T(8,128)(2,1)S(1)}, bf16[64,1024]{1,0:T(8,128)(2,1)}, u32[]{:S(2)}) copy-start(bf16[64,1024]{1,0:T(8,128)(2,1)} %k_ref.1) | copy-start | bytes 393220
  2.1 70.0 %copy-start.7 = (bf16[64,1024]{1,0:T(8,128)(2,1)S(1)}, bf16[64,1024]{1,0:T(8,128)(2,1)}, u32[]{:S(2)}) copy-start(bf16[64,1024]{1,0:T(8,128)(2,1)} %v_ref.1) | copy-start | bytes 393220

commit v5 on v4

--- a/solution.py
+++ b/solution.py
@@ -20,7 +20,6 @@
 LOG2E = 1.4426950408889634
 SCALE = HD**-0.5
 AHEAD = 6
-EARLY = 2
 LAST = (((1,), (1,)), ((), ()))
 FIRST = (((0,), (0,)), ((), ()))
 
@@ -281,13 +280,13 @@
         return jnp.maximum(most, first_count + second_block - first_ref[second_block] + 1)
 
     most_ref[0] = lax.fori_loop(0, CTX, tile_count, 0)
-    drain(kv.at[0], list_recv.at[0])
-
+    take_chunk(2)
     def second_round():
         drain(pieces, piece_recv)
         send_lists()
 
     pl.when(kind == 1)(second_round)
+    drain(kv.at[0], list_recv.at[0])
 
     zeros = jnp.zeros((HD, BLOCK), jnp.bfloat16)
 
@@ -296,14 +295,14 @@
         for i, flag in enumerate((~belongs(t), belongs(t))):
             wide[i * HD : (i + 1) * HD, tile_cols(t)] = jnp.where(flag, turned, zeros)
 
-    unroll = 3 if slots % 3 == 0 else 2
-
-    def tiles(body):
+    def tiles(body, first=0, last=slots):
+        unroll = last - first if slots == SHORT else 2
+
         def several(index):
             for u in range(unroll):
-                body(index * unroll + u)
-
-        loop(slots // unroll, several)
+                body(first + index * unroll + u)
+
+        loop((last - first) // unroll, several)
 
     def tile_cols(t):
         return pl.ds(pl.multiple_of(t * BLOCK, BLOCK), BLOCK)
@@ -377,7 +376,7 @@
             total = jnp.sum(fold(product, jnp.add), axis=0, keepdims=True)
             delta[i] = jnp.broadcast_to(total, (8, BLOCK))
 
-    def value_grad(g, store):
+    def value_grad(g, store, *span):
         def step(t):
             store(
                 t,
@@ -388,9 +387,9 @@
                 ),
             )
 
-        tiles(step)
-
-    def key_grad(g, store):
+        tiles(step, *span)
+
+    def key_grad(g, store, *span):
         def step(t):
             prob_grad = jnp.dot(kv[1, t], turned[chosen(t)], preferred_element_type=jnp.float32)
             score_grad = (
@@ -402,7 +401,7 @@
                 t, jnp.dot(score_grad, q_buf[g, chosen(t)], preferred_element_type=jnp.float32)
             )
 
-        tiles(step)
+        tiles(step, *span)
 
     def query_grad(g):
         both = jnp.dot(wide_keys[...], grads[g], preferred_element_type=jnp.float32)
@@ -453,7 +452,7 @@
 
     loop(slots, functools.partial(widen, wide_keys, 0))
     for g in range(GROUP):
-        if g >= 2:
+        if g >= 3:
             take_chunk(g)
         forward(g)
     for g in range(GROUP - 1):
@@ -468,15 +467,17 @@
         turn(g)
         key_grad(g, keep(0))
 
-    loop(EARLY, early)
-    take_chunk(2 * GROUP - 1)
-    prepare(GROUP - 1)
-    value_grad(GROUP - 1, finish(1, 1.0))
+    last = GROUP - 1
+    take_chunk(GROUP + last)
+    prepare(last)
+    value_grad(last, finish(1, 1.0), 2, slots)
     send_parts(1)
-    loop(GROUP - 1 - EARLY, lambda g: early(g + EARLY))
-    turn(GROUP - 1)
-    key_grad(GROUP - 1, finish(0, SCALE))
+    loop(last, early)
+    turn(last)
+    key_grad(last, finish(0, SCALE), 2, slots)
     send_parts(0)
+    value_grad(last, finish(1, 1.0), 0, 2)
+    key_grad(last, finish(0, SCALE), 0, 2)
     loop(GROUP, query_grad)
 
     nowhere = CTX * others

time: 73.3 us -> 69.4 us (0.947)
  Pallas kernels: 70.5 us -> 66.2 us
    pallas_call x1, Pallas kernels: 69.4 us -> 65.1 us  [fused(): pl.pallas_call(functools.partial(fused_kernel, slots, docs), out_shape=(j...]
where the time goes in v5:
time: 69.4 us; the launch traced here: 69.3 us
  Pallas kernels  66.2 us (95%)
  between operations  1.45 us (2%)
  other arithmetic  0.76 us (1%)
    pallas_call x1, Pallas kernels, fused(): pl.pallas_call(functools.partial(fused_kernel, slots, docs), out_shape=(j...  65.1 us

profile of v5, /device:TPU:1, one launch (start us, length us, event | category | flops | bytes accessed | tf_op | source)
XLA Modules:
  0.0 69.3 jit_solution(1444040107067530542)
XLA Ops:
  0.6 0.8 %select_reduce_fusion.inverse_ref = s32[64]{0:T(128)S(1)} fusion(s32[64]{0:T(128)} %order_ref.1), kind=kLoop, calls=%fused_computation | loop fusion | flops 12224 | bytes 512 | tf_op jit(solution)/shard_map/reduce_sum | solution.py:637
  1.4 0.0 copy-start.8
  1.4 0.0 copy-start.9
  1.4 0.0 copy-start.10
  1.4 0.6 copy-done.8
  2.1 0.0 copy-done.9
  2.1 0.0 copy-done.10
  2.1 0.0 copy-start.4
  2.1 0.0 copy-start.5
  2.1 0.0 copy-start.6
  2.1 0.0 copy-start.7
  2.1 65.1 %fused.3 = (bf16[512,512]{1,0:T(8,128)(2,1)S(1)}, bf16[512,512]{1,0:T(8,128)(2,1)S(1)}, bf16[2,256,128]{2,1,0:T(8,128)(2,1)S(1)}, bf16[2,256,128]{2,1,0:T(8,128)(2,1)S(1)}, s32[1]{0:T(128)}) custom-call(s32[64]{0:T(128)S(1)} %copy-done.8, s32[64]{0:T(128)S(1)} %select_reduce_fusion.inverse_ref, s32[64]{0:T(128)S(1)} %copy-done.9, s32[13]{0:T(128)S(1)} %copy-done.10, ...), custom_call_target="tpu_custom_call" | custom-call | tf_op jit(solution)/shard_map/fused/pallas_call | solution.py:554
  67.8 0.0 copy-done.4
  67.8 0.0 copy-done.5
  67.8 0.0 copy-done.6
  67.8 0.0 copy-done.7
  67.8 1.3 %conditional.1 = ((bf16[512,512]{1,0:T(8,128)(2,1)}, bf16[512,512]{1,0:T(8,128)(2,1)}, bf16[512,128]{1,0:T(8,128)(2,1)}, bf16[512,128]{1,0:T(8,128)(2,1)})) conditional(s32[]{:T(128)} %bitcast.4, (s32[64]{0:T(128)S(1)}, s32[64]{0:T(128)S(1)}, s32[64]{0:T(128)S(1)}, s32[13]{0:T(128)S(1)}, bf16[64,4096]{1,0:T(8,128)(2,1)S(1)}, ...), branch_computations={%region_1.2_spmd, %region_2.3_spmd} | conditional | bytes 5243000 | solution.py:651
  68.0 1.1 %deliver.3 = (bf16[512,512]{1,0:T(8,128)(2,1)}, bf16[512,512]{1,0:T(8,128)(2,1)}, bf16[512,128]{1,0:T(8,128)(2,1)}, bf16[512,128]{1,0:T(8,128)(2,1)}) custom-call(bf16[512,512]{1,0:T(8,128)(2,1)S(1)} %get-tuple-element.36.refs_0_, bf16[512,512]{1,0:T(8,128)(2,1)S(1)} %get-tuple-element.37.refs_1_, bf16[512,128]{1,0:T(8,128)(2,1)S(1)} %bitcast.7, ...), custom_call_target="tpu_custom_call" | custom-call | tf_op jit(solution)/shard_map/cond/branch_1_fun/deliver/pallas_call | solution.py:625
Async XLA Ops:
  1.4 0.7 copy-start.8
  1.4 0.7 copy-start.9
  1.4 0.7 copy-start.10
  2.1 65.7 %copy-start.4 = (bf16[64,4096]{1,0:T(8,128)(2,1)S(1)}, bf16[64,4096]{1,0:T(8,128)(2,1)}, u32[]{:S(2)}) copy-start(bf16[64,4096]{1,0:T(8,128)(2,1)} %q_ref.1) | copy-start | bytes 1572868
  2.1 65.7 %copy-start.5 = (bf16[64,4096]{1,0:T(8,128)(2,1)S(1)}, bf16[64,4096]{1,0:T(8,128)(2,1)}, u32[]{:S(2)}) copy-start(bf16[64,4096]{1,0:T(8,128)(2,1)} %g_ref.1) | copy-start | bytes 1572868
  2.1 65.7 %copy-start.6 = (bf16[64,1024]{1,0:T(8,128)(2,1)S(1)}, bf16[64,1024]{1,0:T(8,128)(2,1)}, u32[]{:S(2)}) copy-start(bf16[64,1024]{1,0:T(8,128)(2,1)} %k_ref.1) | copy-start | bytes 393220
  2.1 65.7 %copy-start.7 = (bf16[64,1024]{1,0:T(8,128)(2,1)S(1)}, bf16[64,1024]{1,0:T(8,128)(2,1)}, u32[]{:S(2)}) copy-start(bf16[64,1024]{1,0:T(8,128)(2,1)} %v_ref.1) | copy-start | bytes 393220
